TPU v7x, 32 devices: a whole 2x2x4 slice. The times are simulated.
32 devices in a mesh: sx: 2 (over x), sy: 4 (over y, core), ta: 4 (over z).
Axes of the slice: x: 2, y: 2, z: 4, core: 2. Of those that a mesh axis runs over, the one named last changes fastest.
Arguments:
- velocity: bfloat16 [3, 256, 8, 1024], P(None, 'ta', 'sx', 'sy'), may hold values from -6 to 6
- seeds_first: int32 [64, 64], replicated, may hold values from -64 to 64
- seeds_merge: int32 [2, 128, 64], replicated, may hold values from -64 to 64
Outputs:
- basis: float32 [64, 5, 8, 1024], P(None, None, 'sx', ('sy', 'ta'))
All inputs are finite; a program needn't handle non-finite values.
Results may differ from a plain program's by a relative error of at most 0.0008.
Values may be sent and summed in bfloat16 or wider, within the bound.
A program may use at most 64 MiB of HBM per device.

v0:
```python
import functools

import jax
import jax.numpy as jnp
from jax import lax
from jax.experimental import pallas as pl
from jax.experimental.pallas import tpu as pltpu
from jax.sharding import PartitionSpec as P

HI = lax.Precision.HIGHEST


def mm(left, right, contract=(1, 0)):
    return lax.dot_general(
        left,
        right,
        (((contract[0],), (contract[1],)), ((), ())),
        precision=HI,
        preferred_element_type=jnp.float32,
    )


def eye(rows, cols):
    return (
        lax.broadcasted_iota(jnp.int32, (rows, cols), 0)
        == lax.broadcasted_iota(jnp.int32, (rows, cols), 1)
    ).astype(jnp.float32)


def inverse_factors(mats):
    n = mats[0].shape[0]
    batch = len(mats)
    tiles = n // 8
    ident = eye(n, n)
    width = 2 * n
    work = [
        [jnp.concatenate([m, ident], axis=1)[8 * i : 8 * i + 8] for i in range(tiles)]
        for m in mats
    ]
    sub = lax.broadcasted_iota(jnp.int32, (8, width), 0)
    done = [[None] * tiles for _ in range(batch)]
    for p in range(tiles):
        cols = [
            [
                [
                    jnp.broadcast_to(work[b][i][:, 8 * p + k : 8 * p + k + 1], (8, width))
                    for i in range(p, tiles)
                ]
                for k in range(8)
            ]
            for b in range(batch)
        ]
        for b in range(batch):
            head = work[b][p]
            rest = [work[b][i] for i in range(p + 1, tiles)]
            scales = jnp.zeros((8, width), jnp.float32)
            for k in range(8):
                pivot = cols[b][k][0][k : k + 1]
                inv = 1.0 / pivot
                scales = jnp.where(sub == k, jnp.broadcast_to(inv, (8, width)), scales)
                row = head[k : k + 1] * inv
                across = [cols[b][j][0][k : k + 1] * inv for j in range(k + 1, 8)]
                below = jnp.where(sub > k, cols[b][k][0], 0.0)
                head = head - below * row
                for j in range(k + 1, 8):
                    cols[b][j][0] = cols[b][j][0] - below * across[j - k - 1]
                for i in range(1, tiles - p):
                    factor = cols[b][k][i]
                    rest[i - 1] = rest[i - 1] - factor * row
                    for j in range(k + 1, 8):
                        cols[b][j][i] = cols[b][j][i] - factor * across[j - k - 1]
            done[b][p] = head * jnp.sqrt(scales)
            for i in range(p + 1, tiles):
                work[b][i] = rest[i - p - 1]
    return [jnp.concatenate(done[b], axis=0)[:, n:] for b in range(batch)]


def solve_steps(grams, rotation):
    order_n = rotation.shape[0]
    ident = eye(order_n, order_n)
    imaged = [mm(g, rotation) for g in grams]
    reduced = [mm(rotation, z, (0, 0)) for z in imaged]
    inverses = inverse_factors(reduced)
    out = []
    for g, z, inverse in zip(grams, imaged, inverses):
        trace = jnp.sum(jnp.sum(g * ident, axis=0, keepdims=True), axis=1, keepdims=True)
        out.append(mm(inverse, z, (1, 1)) * lax.rsqrt(trace / order_n))
    return out


def block_diagonal(low, high):
    zero_low = jnp.zeros((low.shape[0], high.shape[1]), jnp.float32)
    zero_high = jnp.zeros((high.shape[0], low.shape[1]), jnp.float32)
    return jnp.concatenate(
        [
            jnp.concatenate([low, zero_low], axis=1),
            jnp.concatenate([zero_high, high], axis=1),
        ],
        axis=0,
    )


def tree_kernel(gram_ref, strain_ref, first_ref, merge_ref, out_ref):
    width = first_ref.shape[0]
    pair = 2 * width
    gram_low = gram_ref[:pair]
    gram_cross = gram_ref[pair : 2 * pair]
    gram_high = gram_ref[2 * pair : 3 * pair]
    first = eye(width, width) + first_ref[...].astype(jnp.float32) * (0.5 / 512.0)
    stacked = jnp.concatenate([eye(width, width)] * 2, axis=0) * (2.0**-0.5)
    turns = [
        stacked + merge_ref[level].astype(jnp.float32) * (0.5 / (64.0 * 128.0**0.5))
        for level in range(2)
    ]
    coefs = solve_steps(
        [g[i * width : (i + 1) * width, i * width : (i + 1) * width] for g in (gram_low, gram_high) for i in (0, 1)],
        first,
    )
    low, high = block_diagonal(coefs[0], coefs[1]), block_diagonal(coefs[2], coefs[3])
    solved = solve_steps(
        [mm(mm(low, gram_low), low, (1, 1)), mm(mm(high, gram_high), high, (1, 1))], turns[0]
    )
    low, high = mm(solved[0], low), mm(solved[1], high)
    cross = mm(mm(high, gram_cross), low, (1, 1))
    top = jnp.concatenate([mm(mm(low, gram_low), low, (1, 1)), cross.T], axis=1)
    bottom = jnp.concatenate([cross, mm(mm(high, gram_high), high, (1, 1))], axis=1)
    last = solve_steps([jnp.concatenate([top, bottom], axis=0)], turns[1])[0]
    weights = jnp.concatenate([mm(last[:, :width], low), mm(last[:, width:], high)], axis=1)
    out_ref[...] = mm(weights, strain_ref[...])


MESH = pl.DeviceIdType.MESH


def loop(start, stop, body):
    if stop - start <= 8:
        for i in range(start, stop):
            body(i)
    else:
        lax.fori_loop(start, stop, lambda i, carry: (body(i), carry)[1], 0)


def dot16(left, right, contract=(1, 0)):
    return lax.dot_general(
        left,
        right,
        (((contract[0],), (contract[1],)), ((), ())),
        preferred_element_type=jnp.float32,
    )


def iotas(rows, cols):
    return (
        lax.broadcasted_iota(jnp.int32, (rows, cols), 0),
        lax.broadcasted_iota(jnp.int32, (rows, cols), 1),
    )


def signed_half(plus, minus):
    return (0.5 * plus.astype(jnp.float32) - 0.5 * minus.astype(jnp.float32)).astype(jnp.bfloat16)


def gather_kernel(
    quarter, nx, ny, nt,
    velocity_ref, strain_ref, gram_ref,
    chunk_ref, held, from_up, from_down, edges, from_left, from_right, parts, landed, slices, whole,
    chunk_sems, x_sems, y_sems, rim_sems, scatter_sems, line_sems, spread_sems,
):
    ix, iy, it = lax.axis_index("sx"), lax.axis_index("sy"), lax.axis_index("ta")
    plane = nx * ny
    me = ix * ny + iy
    rows3, lanes = chunk_ref.shape[1:]
    snaps = rows3 // 3
    cells_x = lanes // quarter

    def plane_peer(j):
        t = lax.rem(me + j, plane)
        return t, (t // ny, lax.rem(t, ny), it)

    def ta_peer(d):
        t = lax.rem(it + d, nt)
        return t, (ix, iy, t)

    def copy(src, dst, sems, index, device):
        return pltpu.make_async_remote_copy(
            src_ref=src, dst_ref=dst, send_sem=sems.at[0, index], recv_sem=sems.at[1, index],
            device_id=device, device_id_type=MESH,
        )

    barrier = pltpu.get_barrier_semaphore()

    def greet(device):
        pl.semaphore_signal(barrier, inc=1, device_id=device, device_id_type=MESH)

    loop(1, plane, lambda j: greet(plane_peer(j)[1]))
    for d in range(1, nt):
        greet(ta_peer(d)[1])
    right_ok, left_ok = iy + 1 < ny, iy > 0
    first, last = it == 0, it == nt - 1

    @pl.when(jnp.logical_and(right_ok, it > 0))
    def _():
        greet((ix, iy + 1, 0))

    @pl.when(jnp.logical_and(left_ok, it < nt - 1))
    def _():
        greet((ix, iy - 1, nt - 1))

    @pl.when(jnp.logical_and(left_ok, first))
    def _():
        for b in range(1, nt):
            greet((ix, iy - 1, b))

    @pl.when(jnp.logical_and(right_ok, last))
    def _():
        for b in range(nt - 1):
            greet((ix, iy + 1, b))

    extra = (
        jnp.where(right_ok, jnp.where(last, nt - 1, 0) + jnp.where(it > 0, 1, 0), 0)
        + jnp.where(left_ok, jnp.where(first, nt - 1, 0) + jnp.where(it < nt - 1, 1, 0), 0)
    )

    for c in range(3):
        field = velocity_ref[c].astype(jnp.float32)
        rows = [field[:, x, :] for x in range(cells_x)]
        for q in range(nt):
            piece = jnp.concatenate([r[:, q * quarter : (q + 1) * quarter] for r in rows], axis=1)
            chunk_ref[q, c * snaps : (c + 1) * snaps] = piece.astype(jnp.bfloat16)
    pl.semaphore_wait(barrier, plane - 1 + nt - 1 + extra)

    def chunk_copy(d, arriving=False):
        t, device = ta_peer(d)
        slot = lax.rem(it - d + nt, nt) if arriving else it
        return copy(chunk_ref.at[t], held.at[slot], chunk_sems, d, device)

    for d in range(1, nt):
        chunk_copy(d).start()
    held[it] = chunk_ref[it]

    row, lane = iotas(16, lanes)
    column = jnp.where(
        row < cells_x, row * quarter, (row - cells_x) * quarter + quarter - 1
    )
    column = jnp.where(row < 2 * cells_x, column, -1)
    select = (lane == column).astype(jnp.float32).astype(jnp.bfloat16)
    for q in range(nt):
        edges[q] = dot16(select, chunk_ref[q], (1, 1)).astype(jnp.bfloat16)

    def left_copy(d):
        q, device = ta_peer(d)
        return q > 0, copy(edges.at[jnp.maximum(q - 1, 0)], from_left.at[it], y_sems, d, device)

    def right_copy(d):
        q, device = ta_peer(d)
        return q < nt - 1, copy(
            edges.at[jnp.minimum(q + 1, nt - 1)], from_right.at[it], y_sems, nt + d, device
        )

    def rim_copies():
        up = (ix, jnp.minimum(iy + 1, ny - 1), 0)
        down = (ix, jnp.maximum(iy - 1, 0), nt - 1)
        return (
            (right_ok, copy(edges.at[nt - 1], from_left.at[it], rim_sems, it, up)),
            (left_ok, copy(edges.at[0], from_right.at[it], rim_sems, nt + it, down)),
        )

    def each_edge(act):
        for d in range(1, nt):
            for cond, c in (left_copy(d), right_copy(d)):
                pl.when(cond)(functools.partial(act, c))
        for cond, c in rim_copies():
            pl.when(cond)(functools.partial(act, c))

    each_edge(lambda c: c.start())

    @pl.when(it > 0)
    def _():
        from_left[it] = edges[jnp.maximum(it - 1, 0)]

    @pl.when(it < nt - 1)
    def _():
        from_right[it] = edges[jnp.minimum(it + 1, nt - 1)]

    @pl.when(jnp.logical_and(first, jnp.logical_not(left_ok)))
    def _():
        from_left[...] = jnp.zeros_like(from_left)

    @pl.when(jnp.logical_and(last, jnp.logical_not(right_ok)))
    def _():
        from_right[...] = jnp.zeros_like(from_right)

    def x_copies(d):
        b = lax.rem(it - d + nt, nt)
        up = (jnp.minimum(ix + 1, nx - 1), iy, it)
        down = (jnp.maximum(ix - 1, 0), iy, it)
        return (
            (ix < nx - 1, copy(held.at[b, :, pl.ds(lanes - 128, 128)], from_up.at[b], x_sems, d, up)),
            (ix > 0, copy(held.at[b, :, pl.ds(0, 128)], from_down.at[b], x_sems, nt + d, down)),
        )

    @pl.when(ix == 0)
    def _():
        from_up[...] = jnp.zeros_like(from_up)

    @pl.when(ix == nx - 1)
    def _():
        from_down[...] = jnp.zeros_like(from_down)

    for d in range(nt):
        if d:
            chunk_copy(d, True).wait_recv()
        for cond, c in x_copies(d):
            pl.when(cond)(functools.partial(lambda c: c.start(), c))

    row, lane = iotas(lanes, lanes)
    gap = row - lane
    same = row // quarter == lane // quarter
    both = jnp.concatenate(
        [
            signed_half(gap == quarter, gap == -quarter),
            signed_half((gap == 1) & same, (gap == -1) & same),
        ],
        axis=1,
    )
    row, lane = iotas(128, lanes)
    none = row < 0
    above = signed_half(none, (row - (128 - quarter) == lane) & (row >= 128 - quarter))
    below = signed_half((lane - (lanes - quarter) == row) & (row < quarter), none)
    row, lane = iotas(16, lanes)
    none = row < 0
    left = signed_half(
        none, (row >= cells_x) & (row < 2 * cells_x) & (lane == (row - cells_x) * quarter)
    )
    right = signed_half((row < cells_x) & (lane == row * quarter + quarter - 1), none)

    @pl.when(it > 0)
    def _():
        for d in range(1, nt):
            b = lax.rem(it - d + nt, nt)
            copy(edges.at[0], from_left.at[b], y_sems, d, (ix, iy, b)).wait_recv()

    @pl.when(it < nt - 1)
    def _():
        for d in range(1, nt):
            b = lax.rem(it - d + nt, nt)
            copy(edges.at[0], from_right.at[b], y_sems, nt + d, (ix, iy, b)).wait_recv()

    @pl.when(jnp.logical_and(first, left_ok))
    def _():
        for b in range(nt):
            copy(edges.at[0], from_left.at[b], rim_sems, b, (ix, iy - 1, b)).wait_recv()

    @pl.when(jnp.logical_and(last, right_ok))
    def _():
        for b in range(nt):
            copy(edges.at[0], from_right.at[b], rim_sems, nt + b, (ix, iy + 1, b)).wait_recv()

    @pl.when(ix > 0)
    def _():
        for d in range(nt):
            b = lax.rem(it - d + nt, nt)
            copy(
                held.at[b, :, pl.ds(lanes - 128, 128)], from_up.at[b], x_sems, d, (ix - 1, iy, it)
            ).wait_recv()

    @pl.when(ix < nx - 1)
    def _():
        for d in range(nt):
            b = lax.rem(it - d + nt, nt)
            copy(
                held.at[b, :, pl.ds(0, 128)], from_down.at[b], x_sems, nt + d, (ix + 1, iy, it)
            ).wait_recv()

    for b in range(nt):
        inner = dot16(held[b], both)
        dx = inner[:, :lanes] + dot16(from_up[b], above) + dot16(from_down[b], below)
        dy = inner[:, lanes:] + dot16(from_left[b], left, (0, 0)) + dot16(from_right[b], right, (0, 0))
        ux, vx, wx = (dx[i * snaps : (i + 1) * snaps] for i in range(3))
        uy, vy, wy = (dy[i * snaps : (i + 1) * snaps] for i in range(3))
        for k, field in enumerate((ux, vy, 0.5 * (uy + vx), 0.5 * wx, 0.5 * wy)):
            strain_ref[b * snaps : (b + 1) * snaps, k * lanes : (k + 1) * lanes] = field

    strain = strain_ref[...]
    coarse = strain.astype(jnp.bfloat16)
    fine = (strain - coarse.astype(jnp.float32)).astype(jnp.bfloat16)
    half = nt * snaps // 2
    blocks = []
    for a, b in ((0, 0), (1, 0), (1, 1)):
        ra, rb = slice(a * half, (a + 1) * half), slice(b * half, (b + 1) * half)
        blocks.append(
            dot16(coarse[ra], coarse[rb], (1, 1))
            + (dot16(coarse[ra], fine[rb], (1, 1)) + dot16(fine[ra], coarse[rb], (1, 1)))
        )
    share = parts.shape[1]
    spare = plane * share - 3 * half
    if spare:
        blocks.append(jnp.zeros((spare, 128), jnp.float32))
    parts[...] = jnp.concatenate(blocks, axis=0).reshape(plane, share, 128)

    def scatter_copy(j):
        t, device = plane_peer(j)
        return copy(parts.at[t], landed.at[j], scatter_sems, j, device)

    loop(1, plane, lambda j: scatter_copy(j).start())
    landed[0] = parts[me]
    loop(1, plane, lambda j: scatter_copy(j).wait_recv())
    slices[it] = jnp.sum(landed[...], axis=0)

    for d in range(1, nt):
        copy(slices.at[it], slices.at[it], line_sems, d, ta_peer(d)[1]).start()
    for d in range(1, nt):
        b = lax.rem(it - d + nt, nt)
        copy(slices.at[it], slices.at[b], line_sems, d, ta_peer(d)[1]).wait_recv()
    whole[me] = jnp.sum(slices[...], axis=0)

    loop(1, plane, lambda j: copy(whole.at[me], whole.at[me], spread_sems, j, plane_peer(j)[1]).start())

    def arrive(j):
        t = lax.rem(me - j + plane, plane)
        copy(whole.at[me], whole.at[t], spread_sems, j, plane_peer(j)[1]).wait_recv()

    loop(1, plane, arrive)
    gram_ref[...] = whole[...].reshape(plane * share, 128)

    for d in range(1, nt):
        chunk_copy(d).wait_send()
        copy(slices.at[it], slices.at[it], line_sems, d, ta_peer(d)[1]).wait_send()
    each_edge(lambda c: c.wait_send())
    for d in range(nt):
        for cond, c in x_copies(d):
            pl.when(cond)(functools.partial(lambda c: c.wait_send(), c))
    loop(1, plane, lambda j: scatter_copy(j).wait_send())
    loop(1, plane, lambda j: copy(whole.at[me], whole.at[me], spread_sems, j, plane_peer(j)[1]).wait_send())


def local(velocity, seeds_first, seeds_merge):
    comps, width, cells_x, cells_y = velocity.shape
    nx, ny, nt = (lax.axis_size(a) for a in ("sx", "sy", "ta"))
    quarter = cells_y // nt
    lanes = cells_x * quarter
    plane = nx * ny
    share = -(-3 * 2 * width // (8 * plane)) * 8
    rows3 = comps * width
    vmem = pl.BlockSpec(memory_space=pltpu.VMEM)
    b16, f32 = jnp.bfloat16, jnp.float32
    dma = pltpu.SemaphoreType.DMA
    strain, gram = pl.pallas_call(
        functools.partial(gather_kernel, quarter, nx, ny, nt),
        out_shape=(
            jax.ShapeDtypeStruct((nt * width, 5 * lanes), f32),
            jax.ShapeDtypeStruct((plane * share, 128), f32),
        ),
        in_specs=[vmem],
        out_specs=(vmem, vmem),
        scratch_shapes=[
            pltpu.VMEM((nt, rows3, lanes), b16),
            pltpu.VMEM((nt, rows3, lanes), b16),
            pltpu.VMEM((nt, rows3, 128), b16),
            pltpu.VMEM((nt, rows3, 128), b16),
            pltpu.VMEM((nt, 16, rows3), b16),
            pltpu.VMEM((nt, 16, rows3), b16),
            pltpu.VMEM((nt, 16, rows3), b16),
            pltpu.VMEM((plane, share, 128), f32),
            pltpu.VMEM((plane, share, 128), f32),
            pltpu.VMEM((nt, share, 128), f32),
            pltpu.VMEM((plane, share, 128), f32),
            dma((2, nt)),
            dma((2, 2 * nt)),
            dma((2, 2 * nt)),
            dma((2, 2 * nt)),
            dma((2, plane)),
            dma((2, nt)),
            dma((2, plane)),
        ],
        compiler_params=pltpu.CompilerParams(
            collective_id=0, has_side_effects=True, vmem_limit_bytes=32 * 2**20
        ),
        name="gather",
    )(velocity)
    out = pl.pallas_call(
        tree_kernel,
        out_shape=jax.ShapeDtypeStruct((width, 5 * lanes), f32),
        in_specs=[vmem] * 4,
        out_specs=vmem,
        compiler_params=pltpu.CompilerParams(vmem_limit_bytes=32 * 2**20),
        name="tree",
    )(gram, strain, seeds_first, seeds_merge)
    return out.reshape(width, 5, cells_x, quarter)


def solution(mesh):
    in_specs = (P(None, "ta", "sx", "sy"), P(), P())
    out_specs = P(None, None, "sx", ("sy", "ta"))
    return jax.shard_map(local, mesh=mesh, in_specs=in_specs, out_specs=out_specs, check_vma=False)
```

profile of v0, /device:TPU:0, one launch (start us, length us, event | category | flops | bytes accessed | tf_op | source)
XLA Modules:
  0.0 48.8 jit_solution(2943508974476397232)
XLA Ops:
  0.0 0.9 %copy.4.merge_ref = s32[2,128,64]{2,1,0:T(8,128)S(1)} copy(s32[2,128,64]{1,2,0:T(8,128)} %param.5) | data formatting | bytes 131072 | tf_op args[2]
  0.9 0.0 copy-start
  1.0 1.0 %copy-done = bf16[3,64,4,256]{3,2,1,0:T(4,128)(2,1)S(1)} copy-done((bf16[3,64,4,256]{3,2,1,0:T(4,128)(2,1)S(1)}, bf16[3,64,4,256]{3,2,1,0:T(4,128)(2,1)}, u32[]{:S(2)}) %copy-start) | copy-done | bytes 393240
  1.9 34.3 %gather.1 = (f32[256,1280]{1,0:T(8,128)S(1)}, f32[384,128]{1,0:T(8,128)S(1)}) custom-call(bf16[3,64,4,256]{3,2,1,0:T(4,128)(2,1)S(1)} %copy-done), custom_call_target="tpu_custom_call" | custom-call | tf_op jit(solution)/shard_map/gather/pallas_call | solution.py:448
  36.2 0.0 copy-start.1
  36.2 0.7 %copy-done.1 = s32[64,64]{1,0:T(8,128)S(1)} copy-done((s32[64,64]{1,0:T(8,128)S(1)}, s32[64,64]{1,0:T(8,128)}, u32[]{:S(2)}) %copy-start.1) | copy-done | bytes 16408
  37.0 10.7 %tree.1 = f32[64,1280]{1,0:T(8,128)S(1)} custom-call(f32[384,128]{1,0:T(8,128)S(1)} %get-tuple-element.7.gram_ref, f32[256,1280]{1,0:T(8,128)S(1)} %get-tuple-element.8.strain_ref, s32[64,64]{1,0:T(8,128)S(1)} %copy-done.1, s32[2,128,64]{2,1,0:T(8,128)S(1)} %copy.4.merge_ref), custom_call_target="tpu_custom_call" | custom-call | tf_op jit(solution)/shard_map/tree/pallas_call | solution.py:481
  47.7 1.1 %reshape.3 = f32[64,5,4,64]{3,2,1,0:T(4,128)} reshape(f32[64,1280]{1,0:T(8,128)S(1)} %tree.1) | data formatting | bytes 655360 | tf_op jit(solution)/shard_map/reshape | solution.py:489
Async XLA Ops:
  0.9 1.0 %copy-start = (bf16[3,64,4,256]{3,2,1,0:T(4,128)(2,1)S(1)}, bf16[3,64,4,256]{3,2,1,0:T(4,128)(2,1)}, u32[]{:S(2)}) copy-start(bf16[3,64,4,256]{3,2,1,0:T(4,128)(2,1)} %velocity_ref.1) | copy-start | bytes 1179652
  36.2 0.8 %copy-start.1 = (s32[64,64]{1,0:T(8,128)S(1)}, s32[64,64]{1,0:T(8,128)}, u32[]{:S(2)}) copy-start(s32[64,64]{1,0:T(8,128)} %first_ref.1) | copy-start | bytes 49156
where the time goes:
time: 49.1 us; the launch traced here: 48.8 us
  Pallas kernels  45 us (92%)
  local copies, waits for them, and re-layouts  3.8 us (8%)
    pallas_call x1, Pallas kernels, local(): pl.pallas_call(functools.partial(gather_kernel, quarter, nx, ny, nt), out...  34.3 us
    pallas_call x1, Pallas kernels, local(): pl.pallas_call(tree_kernel, out_shape=jax.ShapeDtypeStruct((width, 5 * la...  10.7 us
    unnamed x5, local copies, waits for them, and re-layouts  2.68 us
    reshape x1, local copies, waits for them, and re-layouts, local(): return out.reshape(width, 5, cells_x, quarter)  1.13 us

commit v1 on v0

v1 whole, which is shorter than its diff:
```python
import functools

import jax
import jax.numpy as jnp
from jax import lax
from jax.experimental import pallas as pl
from jax.experimental.pallas import tpu as pltpu
from jax.sharding import PartitionSpec as P

HI = lax.Precision.HIGHEST
MESH = pl.DeviceIdType.MESH
OWNERS = 16


def mm(left, right, contract=(1, 0)):
    return lax.dot_general(
        left,
        right,
        (((contract[0],), (contract[1],)), ((), ())),
        precision=HI,
        preferred_element_type=jnp.float32,
    )


def dot16(left, right, contract=(1, 0)):
    return lax.dot_general(
        left,
        right,
        (((contract[0],), (contract[1],)), ((), ())),
        preferred_element_type=jnp.float32,
    )


def iotas(rows, cols):
    return (
        lax.broadcasted_iota(jnp.int32, (rows, cols), 0),
        lax.broadcasted_iota(jnp.int32, (rows, cols), 1),
    )


def eye(rows, cols):
    row, col = iotas(rows, cols)
    return (row == col).astype(jnp.float32)


def signed_half(plus, minus):
    return (0.5 * plus.astype(jnp.float32) - 0.5 * minus.astype(jnp.float32)).astype(jnp.bfloat16)


def eliminate(mats, sides):
    n = mats[0].shape[0]
    batch = len(mats)
    tiles = n // 8
    width = 2 * n
    work = [
        [jnp.concatenate([m, s], axis=1)[8 * i : 8 * i + 8] for i in range(tiles)]
        for m, s in zip(mats, sides)
    ]
    sub = lax.broadcasted_iota(jnp.int32, (8, width), 0)
    done = [[None] * tiles for _ in range(batch)]
    for p in range(tiles):
        cols = [
            [
                [
                    jnp.broadcast_to(work[b][i][:, 8 * p + k : 8 * p + k + 1], (8, width))
                    for i in range(p, tiles)
                ]
                for k in range(8)
            ]
            for b in range(batch)
        ]
        for b in range(batch):
            head = work[b][p]
            rest = [work[b][i] for i in range(p + 1, tiles)]
            scales = jnp.zeros((8, width), jnp.float32)
            for k in range(8):
                pivot = cols[b][k][0][k : k + 1]
                inv = 1.0 / pivot
                scales = jnp.where(sub == k, jnp.broadcast_to(inv, (8, width)), scales)
                row = head[k : k + 1] * inv
                across = [cols[b][j][0][k : k + 1] * inv for j in range(k + 1, 8)]
                below = jnp.where(sub > k, cols[b][k][0], 0.0)
                head = head - below * row
                for j in range(k + 1, 8):
                    cols[b][j][0] = cols[b][j][0] - below * across[j - k - 1]
                for i in range(1, tiles - p):
                    factor = cols[b][k][i]
                    rest[i - 1] = rest[i - 1] - factor * row
                    for j in range(k + 1, 8):
                        cols[b][j][i] = cols[b][j][i] - factor * across[j - k - 1]
            done[b][p] = head * jnp.sqrt(scales)
            for i in range(p + 1, tiles):
                work[b][i] = rest[i - p - 1]
    return [jnp.concatenate(done[b], axis=0)[:, n:] for b in range(batch)]


def total(entries):
    return jnp.sum(jnp.sum(entries, axis=0, keepdims=True), axis=1, keepdims=True)


def first_level(grams, first):
    width = first.shape[0]
    ident = eye(width, width)
    images = [mm(first, g, (0, 0)) for g in grams]
    reduced = [mm(z, first) for z in images]
    solved = eliminate(reduced, images)
    return [c * lax.rsqrt(total(g * ident) / width) for c, g in zip(solved, grams)]


def middle_level(pairs, coefs, turn):
    width = turn.shape[0]
    ident = eye(width, width)
    reduced, sides, scales = [], [], []
    for gram, (low, high) in zip(pairs, coefs):
        lean = jnp.concatenate(
            [mm(low, turn[:, :width], (0, 1)), mm(high, turn[:, width:], (0, 1))], axis=0
        )
        image = mm(lean, gram, (0, 0))
        reduced.append(mm(image, lean))
        norms = [mm(c, c, (0, 0)) for c in (low, high)]
        sides.append(
            jnp.concatenate([mm(image[:, :width], norms[0]), mm(image[:, width:], norms[1])], axis=1)
        )
        trace = total(norms[0] * gram[:width, :width]) + total(norms[1] * gram[width:, width:])
        scales.append(lax.rsqrt(trace / (2 * width)))
    inverses = eliminate(reduced, [ident] * len(pairs))
    return [mm(inv, s) * k for inv, s, k in zip(inverses, sides, scales)]


def last_level(pairs, cross, weights, turn):
    width = turn.shape[0]
    lean = [mm(weights[u], turn[:, u * width : (u + 1) * width], (0, 1)) for u in (0, 1)]
    image = [mm(lean[u], pairs[u], (0, 0)) for u in (0, 1)]
    norms = [mm(weights[u], weights[u], (0, 0)) for u in (0, 1)]
    up = mm(lean[1], cross, (0, 0))
    down = mm(lean[0], cross, (0, 1))
    mixed = mm(up, lean[0])
    reduced = mm(image[0], lean[0]) + mm(image[1], lean[1]) + (mixed + mixed.T)
    trace = total(norms[0] * pairs[0]) + total(norms[1] * pairs[1])
    sides = jnp.concatenate([mm(image[0] + up, norms[0]), mm(image[1] + down, norms[1])], axis=1)
    inverse = eliminate([reduced], [eye(width, width)])[0]
    return mm(inverse, sides) * lax.rsqrt(trace / (2 * width))


def gather_kernel(
    quarter, nx, ny, nt,
    velocity_hbm, first_hbm, merge_hbm,
    coarse_ref, fine_ref, weight_ref,
    velocity, seeds_first, seeds_merge, chunk, edge_low, edge_high, column, rim_out,
    rims, land_pair, land_far, column_pair, column_far, halo,
    side_coarse, side_fine, parts_pair, parts_cross, landed_pair, landed_cross, whole_pair, whole_cross,
    load_sems, chunk_sems, column_sems, rim_sems, low_sems, high_sems,
    scatter_sems, scatter_in, spread_sems, spread_in,
):
    ix, iy, it = lax.axis_index("sx"), lax.axis_index("sy"), lax.axis_index("ta")
    plane = nx * ny
    devices = plane * nt
    place = ix * ny + iy
    me = it * plane + place
    rows3, lanes = chunk.shape[1:]
    snaps = rows3 // 3
    cells_x = lanes // quarter
    half3 = rows3 // 2
    odd, upper = lax.rem(it, 2), lax.div(it, 2)
    partner = it + 1 - 2 * odd
    near, far = lax.rem(it + 2, 4), 3 - it
    b16, f32 = jnp.bfloat16, jnp.float32

    def device(t):
        where = lax.rem(t, plane)
        return (lax.div(where, ny), lax.rem(where, ny), lax.div(t, plane))

    def copy(src, dst, send, recv, target):
        return pltpu.make_async_remote_copy(
            src_ref=src, dst_ref=dst, send_sem=send, recv_sem=recv, device_id=target, device_id_type=MESH
        )

    loads = [
        pltpu.make_async_copy(src, dst, load_sems.at[i])
        for i, (src, dst) in enumerate(
            ((velocity_hbm, velocity), (first_hbm, seeds_first), (merge_hbm, seeds_merge))
        )
    ]
    for c in loads:
        c.start()

    barrier = pltpu.get_barrier_semaphore()

    def greet(target):
        pl.semaphore_signal(barrier, inc=1, device_id=target, device_id_type=MESH)

    def greet_plane(j, carry):
        t = lax.rem(place + j, plane)
        greet((lax.div(t, ny), lax.rem(t, ny), it))
        return carry

    others = (partner, near, far)
    for t in others:
        greet((ix, iy, t))
    can_up, can_down = ix < nx - 1, ix > 0
    for ok, step in ((can_up, 1), (can_down, -1)):
        @pl.when(ok)
        def _():
            for t in others:
                greet((ix + step, iy, t))
    lax.fori_loop(1, plane, greet_plane, 0)
    expected = plane - 1 + 3 + jnp.where(can_up, 3, 0) + jnp.where(can_down, 3, 0)

    right_ok, left_ok = iy + 1 < ny, iy > 0

    @pl.when(jnp.logical_not(can_down))
    def _():
        halo[:, :, :128] = jnp.zeros((6, half3, 128), b16)

    @pl.when(jnp.logical_not(can_up))
    def _():
        halo[:, :, 128:] = jnp.zeros((6, half3, 128), b16)

    @pl.when(jnp.logical_not(left_ok))
    def _():
        rims[0] = jnp.zeros((16, rows3), b16)

    @pl.when(jnp.logical_not(right_ok))
    def _():
        rims[1] = jnp.zeros((16, rows3), b16)

    row, lane = iotas(16, lanes)
    pick_right = ((row < cells_x) & (lane == row * quarter + quarter - 1)).astype(f32).astype(b16)
    pick_left = (
        ((row >= cells_x) & (row < 2 * cells_x) & (lane == (row - cells_x) * quarter))
        .astype(f32)
        .astype(b16)
    )

    order = (0, 2, 1, 3)
    loads[0].wait()
    for c in range(3):
        field = velocity[c].astype(f32)
        rows = [field[:, x, :] for x in range(cells_x)]
        for q in range(nt):
            cut = slice(q * quarter, (q + 1) * quarter)
            piece = jnp.concatenate([r[:, cut] for r in rows], axis=1)
            chunk[order[q], c * snaps : (c + 1) * snaps] = piece.astype(b16)
    for q in range(nt):
        whole_piece = chunk[order[q]].astype(f32)
        first_row = whole_piece[:, :quarter]
        last_row = whole_piece[:, lanes - quarter :]
        edge_low[order[q]] = jnp.concatenate([first_row[:half3], first_row[half3:]], axis=1).astype(b16)
        edge_high[order[q]] = jnp.concatenate([last_row[:half3], last_row[half3:]], axis=1).astype(b16)
    right_of = [dot16(pick_right, chunk[order[q]], (1, 1)) for q in range(nt)]
    left_of = [dot16(pick_left, chunk[order[q]], (1, 1)) for q in range(nt)]
    rim_out[0] = right_of[nt - 1].astype(b16)
    rim_out[1] = left_of[0].astype(b16)
    for q in (1, 2):
        column[order[q]] = (right_of[q - 1] + left_of[q + 1]).astype(b16)

    pl.semaphore_wait(barrier, expected)

    mine2, theirs2 = 2 * odd, 2 - 2 * odd
    spot_near, spot_far = 2 * odd + lax.div(near, 2), 2 - 2 * odd + lax.div(far, 2)

    def chunk_copies():
        return (
            copy(chunk.at[pl.ds(theirs2, 2)], land_pair, chunk_sems.at[0, 0], chunk_sems.at[1, 0], (ix, iy, partner)),
            copy(chunk.at[spot_near], land_far.at[0], chunk_sems.at[0, 1], chunk_sems.at[1, 1], (ix, iy, near)),
            copy(chunk.at[spot_far], land_far.at[1], chunk_sems.at[0, 2], chunk_sems.at[1, 2], (ix, iy, far)),
        )

    def column_copies():
        return (
            copy(column.at[pl.ds(theirs2, 2)], column_pair, column_sems.at[0, 0], column_sems.at[1, 0], (ix, iy, partner)),
            copy(column.at[spot_near], column_far.at[0], column_sems.at[0, 1], column_sems.at[1, 1], (ix, iy, near)),
            copy(column.at[spot_far], column_far.at[1], column_sems.at[0, 2], column_sems.at[1, 2], (ix, iy, far)),
        )

    def edge_copies(source, side, sems, to_x):
        at = pl.ds(128 * side, 128)
        return (
            copy(source.at[pl.ds(mine2, 2)], halo.at[pl.ds(0, 2), :, at], sems.at[0, 0], sems.at[1, 0], (to_x, iy, it)),
            copy(source.at[pl.ds(theirs2, 2)], halo.at[pl.ds(2, 2), :, at], sems.at[0, 1], sems.at[1, 1], (to_x, iy, partner)),
            copy(source.at[spot_near], halo.at[4, :, at], sems.at[0, 2], sems.at[1, 2], (to_x, iy, near)),
            copy(source.at[spot_far], halo.at[5, :, at], sems.at[0, 3], sems.at[1, 3], (to_x, iy, far)),
        )

    def rim_copies():
        return (
            (right_ok, copy(rim_out.at[0], rims.at[0], rim_sems.at[0, 0], rim_sems.at[1, 0], (ix, jnp.minimum(iy + 1, ny - 1), it))),
            (left_ok, copy(rim_out.at[1], rims.at[1], rim_sems.at[0, 1], rim_sems.at[1, 1], (ix, jnp.maximum(iy - 1, 0), it))),
        )

    highs = edge_copies(edge_high, 0, high_sems, jnp.minimum(ix + 1, nx - 1))
    lows = edge_copies(edge_low, 1, low_sems, jnp.maximum(ix - 1, 0))

    def edges(index, act):
        pl.when(can_up)(functools.partial(act, highs[index]))
        pl.when(can_down)(functools.partial(act, lows[index]))

    def start(c):
        c.start()

    for ok, c in rim_copies():
        pl.when(ok)(functools.partial(start, c))
    chunk_copies()[0].start()
    edges(1, start)
    edges(0, start)
    chunk_copies()[1].start()
    chunk_copies()[2].start()
    edges(2, start)
    edges(3, start)

    def halo_wait(index):
        pl.when(can_down)(lambda: highs[index].wait_recv())
        pl.when(can_up)(lambda: lows[index].wait_recv())

    pl.when(left_ok)(lambda: rim_copies()[0][1].wait_recv())
    pl.when(right_ok)(lambda: rim_copies()[1][1].wait_recv())
    column[order[0]] = (rims[0].astype(f32) + left_of[1]).astype(b16)
    column[order[nt - 1]] = (right_of[nt - 2] + rims[1].astype(f32)).astype(b16)
    for c in column_copies():
        c.start()

    row, lane = iotas(lanes, lanes)
    gap = row - lane
    same = row // quarter == lane // quarter
    both = jnp.concatenate(
        [
            signed_half(gap == quarter, gap == -quarter),
            signed_half((gap == 1) & same, (gap == -1) & same),
        ],
        axis=1,
    )
    row, lane = iotas(256, 2 * lanes)
    wide, at = lane // lanes, lax.rem(lane, lanes)
    rise, k = row // 128, lax.rem(row, 128)
    hit = k // quarter == wide
    k = lax.rem(k, quarter)
    outer = signed_half(
        hit & (rise == 1) & (at == k + lanes - quarter), hit & (rise == 0) & (at == k)
    )
    row, lane = iotas(16, lanes)
    rim = signed_half(
        (row >= cells_x) & (row < 2 * cells_x) & (lane == (row - cells_x) * quarter + quarter - 1),
        (row < cells_x) & (lane == row * quarter),
    )

    def strain(block, border, sides):
        inner = dot16(block, both)
        across = dot16(border, outer)
        dx = inner[:, :lanes] + jnp.concatenate([across[:, :lanes], across[:, lanes:]], axis=0)
        dy = inner[:, lanes:] + dot16(sides, rim, (0, 0))
        ux, vx, wx = (dx[i * snaps : (i + 1) * snaps] for i in range(3))
        uy, vy, wy = (dy[i * snaps : (i + 1) * snaps] for i in range(3))
        fields = jnp.concatenate([ux, vy, 0.5 * (uy + vx), 0.5 * wx, 0.5 * wy], axis=1)
        coarse = fields.astype(b16)
        return coarse, (fields - coarse.astype(f32)).astype(b16)

    def keep(block, values):
        at = pl.ds(pl.multiple_of(block * snaps, snaps), snaps)
        coarse_ref[at], fine_ref[at] = values

    def keep_side(block, values):
        at = pl.ds(pl.multiple_of(block * snaps, snaps), snaps)
        side_coarse[at], side_fine[at] = values

    halo_wait(0)
    keep(it, strain(chunk[mine2 + upper], halo[upper], column[mine2 + upper]))
    keep_side(odd, strain(chunk[mine2 + 1 - upper], halo[1 - upper], column[mine2 + 1 - upper]))
    chunk_copies()[0].wait_recv()
    halo_wait(1)
    column_copies()[0].wait_recv()
    keep(partner, strain(land_pair[upper], halo[2 + upper], column_pair[upper]))
    keep_side(1 - odd, strain(land_pair[1 - upper], halo[3 - upper], column_pair[1 - upper]))

    pair = 2 * snaps
    at = pl.ds(pl.multiple_of(upper * pair, pair), pair)
    coarse, fine = coarse_ref[at], fine_ref[at]
    gram = dot16(coarse, jnp.concatenate([coarse, fine], axis=0), (1, 1))
    coarse, fine = side_coarse[...], side_fine[...]
    gram = gram + dot16(coarse, jnp.concatenate([coarse, fine], axis=0), (1, 1))
    skew = gram[:, pair:]
    parts_pair[...] = (gram[:, :pair] + (skew + skew.T)).reshape(OWNERS, 8, pair)

    near_rank = odd * plane + place
    wide_rank = lax.rem(it + 3, 4) * plane + place

    def pair_owner(k):
        return (lax.div(lax.rem(k, plane), ny), lax.rem(lax.rem(k, plane), ny), 2 * upper + lax.div(k, plane))

    def cross_owner(k):
        return (lax.div(lax.rem(k, plane), ny), lax.rem(lax.rem(k, plane), ny), lax.rem(lax.div(k, plane) + 1, 4))

    def scatter(level, act):
        rank, owner, parts, landed = (
            (near_rank, pair_owner, parts_pair, landed_pair),
            (wide_rank, cross_owner, parts_cross, landed_cross),
        )[level]
        for j in range(OWNERS):
            k = lax.rem(rank + j, OWNERS)
            c = copy(parts.at[k], landed.at[rank], scatter_sems.at[level, j], scatter_in.at[level], owner(k))
            if j:
                act(c)
            else:
                pl.when(rank >= OWNERS)(functools.partial(act, c))

    def spread(level, act):
        rank, whole = ((near_rank, whole_pair), (wide_rank, whole_cross))[level]
        slot = jnp.minimum(rank, OWNERS - 1) + (0 if level else OWNERS * upper)

        def body(j, carry):
            act(
                copy(
                    whole.at[slot], whole.at[slot], spread_sems.at[level, j], spread_in.at[level],
                    device(lax.rem(me + j, devices)),
                )
            )
            return carry

        @pl.when(rank < OWNERS)
        def _():
            lax.fori_loop(1, devices, body, 0)

    def reduce(level):
        rank, parts, landed = (
            (near_rank, parts_pair, landed_pair),
            (wide_rank, parts_cross, landed_cross),
        )[level]
        members = landed.shape[0]
        slot = jnp.minimum(rank, OWNERS - 1)

        @pl.when(rank < OWNERS)
        def _():
            landed[rank] = parts[slot]
            some = landed.at[pl.ds(0, members - 1)]
            copy(some, some, scatter_sems.at[level, 0], scatter_in.at[level], (ix, iy, partner)).wait_recv()
            summed = jnp.sum(landed[...], axis=0)
            if level:
                whole_cross[slot] = summed
            else:
                whole_pair[OWNERS * upper + slot] = summed

        spread(level, start)

    scatter(0, start)

    for i, t in enumerate((near, far)):
        chunk_copies()[1 + i].wait_recv()
        halo_wait(2 + i)
        column_copies()[1 + i].wait_recv()
        keep(t, strain(land_far[i], halo[4 + i], column_far[i]))
    coarse, fine = coarse_ref[:pair], fine_ref[:pair]
    coarse_high, fine_high = coarse_ref[pair:], fine_ref[pair:]
    gram = dot16(coarse_high, jnp.concatenate([coarse, fine], axis=0), (1, 1))
    crossed = gram[:, :pair] + (gram[:, pair:] + dot16(fine_high, coarse, (1, 1)))
    parts_cross[...] = crossed.reshape(OWNERS, 8, pair)
    scatter(1, start)
    reduce(0)
    reduce(1)

    for c in loads[1:]:
        c.wait()
    first = eye(snaps, snaps) + seeds_first[...].astype(f32) * (0.5 / 512.0)
    stacked = jnp.concatenate([eye(snaps, snaps)] * 2, axis=1) * (2.0**-0.5)
    turns = [
        stacked + seeds_merge[level].astype(f32) * (0.5 / (64.0 * 128.0**0.5)) for level in range(2)
    ]

    @pl.when(near_rank < OWNERS)
    def _():
        some = whole_pair.at[pl.ds(0, 2 * OWNERS - 1)]
        copy(some, some, spread_sems.at[0, 0], spread_in.at[0], (ix, iy, partner)).wait_recv()

    @pl.when(near_rank >= OWNERS)
    def _():
        copy(whole_pair, whole_pair, spread_sems.at[0, 0], spread_in.at[0], (ix, iy, partner)).wait_recv()

    pairs = [whole_pair[u * OWNERS : (u + 1) * OWNERS].reshape(pair, pair) for u in (0, 1)]
    blocks = [
        g[i * snaps : (i + 1) * snaps, i * snaps : (i + 1) * snaps] for g in pairs for i in (0, 1)
    ]
    coefs = first_level(blocks, first)
    weights = middle_level(pairs, (coefs[:2], coefs[2:]), turns[0])

    @pl.when(wide_rank < OWNERS)
    def _():
        some = whole_cross.at[pl.ds(0, OWNERS - 1)]
        copy(some, some, spread_sems.at[1, 0], spread_in.at[1], (ix, iy, partner)).wait_recv()

    @pl.when(wide_rank >= OWNERS)
    def _():
        copy(whole_cross, whole_cross, spread_sems.at[1, 0], spread_in.at[1], (ix, iy, partner)).wait_recv()

    weight_ref[...] = last_level(pairs, whole_cross[...].reshape(pair, pair), weights, turns[1])

    def finish(c):
        c.wait_send()

    for ok, c in rim_copies():
        pl.when(ok)(functools.partial(finish, c))
    for c in chunk_copies() + column_copies():
        finish(c)
    for index in range(4):
        edges(index, finish)
    for level in range(2):
        scatter(level, finish)
        spread(level, finish)


def tail_kernel(weight_ref, coarse_ref, fine_ref, out_hbm, out, sem):
    modes, lanes = weight_ref.shape[0], coarse_ref.shape[1]
    weights = weight_ref[...]
    coarse = weights.astype(jnp.bfloat16)
    fine = (weights - coarse.astype(jnp.float32)).astype(jnp.bfloat16)
    both = dot16(jnp.concatenate([coarse, fine], axis=0), coarse_ref[...])
    basis = both[:modes] + (both[modes:] + dot16(coarse, fine_ref[...]))
    quarter = out.shape[1]
    strips = lanes // quarter
    for i in range(strips):
        out[pl.ds(i, modes, stride=strips), :] = basis[:, i * quarter : (i + 1) * quarter]
    done = pltpu.make_async_copy(out, out_hbm, sem)
    done.start()
    done.wait()


def local(velocity, seeds_first, seeds_merge):
    comps, width, cells_x, cells_y = velocity.shape
    nx, ny, nt = (lax.axis_size(a) for a in ("sx", "sy", "ta"))
    quarter = cells_y // nt
    lanes = cells_x * quarter
    plane = nx * ny
    rows3 = comps * width
    pair = 2 * width
    vmem = pl.BlockSpec(memory_space=pltpu.VMEM)
    hbm = pl.BlockSpec(memory_space=pltpu.HBM)
    b16, f32 = jnp.bfloat16, jnp.float32
    dma = pltpu.SemaphoreType.DMA
    coarse, fine, weights = pl.pallas_call(
        functools.partial(gather_kernel, quarter, nx, ny, nt),
        out_shape=(
            jax.ShapeDtypeStruct((nt * width, 5 * lanes), b16),
            jax.ShapeDtypeStruct((nt * width, 5 * lanes), b16),
            jax.ShapeDtypeStruct((width, nt * width), f32),
        ),
        in_specs=[hbm] * 3,
        out_specs=(vmem,) * 3,
        scratch_shapes=[
            pltpu.VMEM(velocity.shape, b16),
            pltpu.VMEM((width, width), jnp.int32),
            pltpu.VMEM((2, width, pair), jnp.int32),
            pltpu.VMEM((nt, rows3, lanes), b16),
            pltpu.VMEM((nt, rows3 // 2, 128), b16),
            pltpu.VMEM((nt, rows3 // 2, 128), b16),
            pltpu.VMEM((nt, 16, rows3), b16),
            pltpu.VMEM((2, 16, rows3), b16),
            pltpu.VMEM((2, 16, rows3), b16),
            pltpu.VMEM((2, rows3, lanes), b16),
            pltpu.VMEM((2, rows3, lanes), b16),
            pltpu.VMEM((2, 16, rows3), b16),
            pltpu.VMEM((2, 16, rows3), b16),
            pltpu.VMEM((6, rows3 // 2, 256), b16),
            pltpu.VMEM((pair, 5 * lanes), b16),
            pltpu.VMEM((pair, 5 * lanes), b16),
            pltpu.VMEM((OWNERS, 8, pair), f32),
            pltpu.VMEM((OWNERS, 8, pair), f32),
            pltpu.VMEM((2 * plane, 8, pair), f32),
            pltpu.VMEM((nt * plane, 8, pair), f32),
            pltpu.VMEM((2 * OWNERS, 8, pair), f32),
            pltpu.VMEM((OWNERS, 8, pair), f32),
            dma((3,)),
            dma((2, 3)),
            dma((2, 3)),
            dma((2, 2)),
            dma((2, 4)),
            dma((2, 4)),
            dma((2, OWNERS)),
            dma((2,)),
            dma((2, nt * plane)),
            dma((2,)),
        ],
        compiler_params=pltpu.CompilerParams(
            collective_id=0, has_side_effects=True, vmem_limit_bytes=40 * 2**20
        ),
        name="gather",
    )(*(pltpu.with_memory_space_constraint(a, pltpu.HBM) for a in (velocity, seeds_first, seeds_merge.transpose(0, 2, 1))))
    strips = 5 * cells_x
    out = pl.pallas_call(
        tail_kernel,
        out_shape=jax.ShapeDtypeStruct((width * strips, quarter), f32),
        in_specs=[vmem] * 3,
        out_specs=hbm,
        scratch_shapes=[pltpu.VMEM((width * strips, quarter), f32), dma],
        compiler_params=pltpu.CompilerParams(vmem_limit_bytes=32 * 2**20),
        name="tail",
    )(weights, coarse, fine)
    return out.reshape(width, 5, cells_x, quarter)


def solution(mesh):
    in_specs = (P(None, "ta", "sx", "sy"), P(), P())
    out_specs = P(None, None, "sx", ("sy", "ta"))
    return jax.shard_map(local, mesh=mesh, in_specs=in_specs, out_specs=out_specs, check_vma=False)
```

time: 49.1 us -> 40.9 us (0.83)
  Pallas kernels: 45 us -> 40.8 us
  local copies, waits for them, and re-layouts: 3.8 us -> 0 us
    pallas_call x1, Pallas kernels: 10.7 us -> 1.26 us  [local(): pl.pallas_call(tail_kernel, out_shape=jax.ShapeDtypeStruct((width * strip...]
    pallas_call x1, Pallas kernels: 34.3 us -> 39.5 us  [local(): pl.pallas_call(functools.partial(gather_kernel, quarter, nx, ny, nt), out...]
    unnamed x5 -> x0, local copies, waits for them, and re-layouts: 2.68 us -> none
    reshape x1 -> x0, local copies, waits for them, and re-layouts: 1.13 us -> none  [local(): return out.reshape(width, 5, cells_x, quarter)]
where the time goes in v1:
time: 40.9 us; the launch traced here: 40.8 us
  Pallas kernels  40.8 us (100%)
    pallas_call x1, Pallas kernels, local(): pl.pallas_call(functools.partial(gather_kernel, quarter, nx, ny, nt), out...  39.5 us
    pallas_call x1, Pallas kernels, local(): pl.pallas_call(tail_kernel, out_shape=jax.ShapeDtypeStruct((width * strip...  1.26 us

profile of v1, /device:TPU:0, one launch (start us, length us, event | category | flops | bytes accessed | tf_op | source)
XLA Modules:
  0.0 40.8 jit_solution(5302863712775512291)
XLA Ops:
  0.0 39.5 %gather.1 = (bf16[256,1280]{1,0:T(8,128)(2,1)S(1)}, bf16[256,1280]{1,0:T(8,128)(2,1)S(1)}, f32[64,256]{1,0:T(8,128)S(1)}) custom-call(bf16[3,64,4,256]{3,2,1,0:T(4,128)(2,1)} %velocity_hbm.1, s32[64,64]{1,0:T(8,128)} %first_hbm.1, s32[2,64,128]{2,1,0:T(8,128)} %bitcast.2), custom_call_target="tpu_custom_call" | custom-call | tf_op jit(solution)/shard_map/gather/pallas_call | solution.py:536
  39.5 1.3 %tail.1 = f32[1280,64]{1,0:T(8,128)} custom-call(f32[64,256]{1,0:T(8,128)S(1)} %get-tuple-element.8.weight_ref, bf16[256,1280]{1,0:T(8,128)(2,1)S(1)} %get-tuple-element.9.coarse_ref, bf16[256,1280]{1,0:T(8,128)(2,1)S(1)} %get-tuple-element.10.fine_ref), custom_call_target="tpu_custom_call" | custom-call | tf_op jit(solution)/shard_map/tail/pallas_call | solution.py:585

commit v2 on v1

--- a/solution.py
+++ b/solution.py
@@ -9,7 +9,7 @@
 
 HI = lax.Precision.HIGHEST
 MESH = pl.DeviceIdType.MESH
-OWNERS = 16
+OWNERS = 24
 
 
 def mm(left, right, contract=(1, 0)):
@@ -147,10 +147,10 @@
     velocity_hbm, first_hbm, merge_hbm,
     coarse_ref, fine_ref, weight_ref,
     velocity, seeds_first, seeds_merge, chunk, edge_low, edge_high, column, rim_out,
-    rims, land_pair, land_far, column_pair, column_far, halo,
-    side_coarse, side_fine, parts_pair, parts_cross, landed_pair, landed_cross, whole_pair, whole_cross,
+    rims, land, column_in, halo_own, halo,
+    own_coarse, own_fine, own_landed, shared, parts, landed, whole,
     load_sems, chunk_sems, column_sems, rim_sems, low_sems, high_sems,
-    scatter_sems, scatter_in, spread_sems, spread_in,
+    own_sems, own_in, share_sems, share_in, scatter_sems, scatter_in, spread_sems, spread_in,
 ):
     ix, iy, it = lax.axis_index("sx"), lax.axis_index("sy"), lax.axis_index("ta")
     plane = nx * ny
@@ -161,8 +161,7 @@
     snaps = rows3 // 3
     cells_x = lanes // quarter
     half3 = rows3 // 2
-    odd, upper = lax.rem(it, 2), lax.div(it, 2)
-    partner = it + 1 - 2 * odd
+    partner = it + 1 - 2 * lax.rem(it, 2)
     near, far = lax.rem(it + 2, 4), 3 - it
     b16, f32 = jnp.bfloat16, jnp.float32
 
@@ -210,11 +209,13 @@
 
     @pl.when(jnp.logical_not(can_down))
     def _():
-        halo[:, :, :128] = jnp.zeros((6, half3, 128), b16)
+        halo[:, :, :128] = jnp.zeros((3, half3, 128), b16)
+        halo_own[:, :, :128] = jnp.zeros((nt, half3, 128), b16)
 
     @pl.when(jnp.logical_not(can_up))
     def _():
-        halo[:, :, 128:] = jnp.zeros((6, half3, 128), b16)
+        halo[:, :, 128:] = jnp.zeros((3, half3, 128), b16)
+        halo_own[:, :, 128:] = jnp.zeros((nt, half3, 128), b16)
 
     @pl.when(jnp.logical_not(left_ok))
     def _():
@@ -232,7 +233,6 @@
         .astype(b16)
     )
 
-    order = (0, 2, 1, 3)
     loads[0].wait()
     for c in range(3):
         field = velocity[c].astype(f32)
@@ -240,47 +240,38 @@
         for q in range(nt):
             cut = slice(q * quarter, (q + 1) * quarter)
             piece = jnp.concatenate([r[:, cut] for r in rows], axis=1)
-            chunk[order[q], c * snaps : (c + 1) * snaps] = piece.astype(b16)
+            chunk[q, c * snaps : (c + 1) * snaps] = piece.astype(b16)
     for q in range(nt):
-        whole_piece = chunk[order[q]].astype(f32)
+        whole_piece = chunk[q].astype(f32)
         first_row = whole_piece[:, :quarter]
         last_row = whole_piece[:, lanes - quarter :]
-        edge_low[order[q]] = jnp.concatenate([first_row[:half3], first_row[half3:]], axis=1).astype(b16)
-        edge_high[order[q]] = jnp.concatenate([last_row[:half3], last_row[half3:]], axis=1).astype(b16)
-    right_of = [dot16(pick_right, chunk[order[q]], (1, 1)) for q in range(nt)]
-    left_of = [dot16(pick_left, chunk[order[q]], (1, 1)) for q in range(nt)]
+        edge_low[q] = jnp.concatenate([first_row[:half3], first_row[half3:]], axis=1).astype(b16)
+        edge_high[q] = jnp.concatenate([last_row[:half3], last_row[half3:]], axis=1).astype(b16)
+    right_of = [dot16(pick_right, chunk[q], (1, 1)) for q in range(nt)]
+    left_of = [dot16(pick_left, chunk[q], (1, 1)) for q in range(nt)]
     rim_out[0] = right_of[nt - 1].astype(b16)
     rim_out[1] = left_of[0].astype(b16)
     for q in (1, 2):
-        column[order[q]] = (right_of[q - 1] + left_of[q + 1]).astype(b16)
+        column[q] = (right_of[q - 1] + left_of[q + 1]).astype(b16)
 
     pl.semaphore_wait(barrier, expected)
 
-    mine2, theirs2 = 2 * odd, 2 - 2 * odd
-    spot_near, spot_far = 2 * odd + lax.div(near, 2), 2 - 2 * odd + lax.div(far, 2)
-
-    def chunk_copies():
-        return (
-            copy(chunk.at[pl.ds(theirs2, 2)], land_pair, chunk_sems.at[0, 0], chunk_sems.at[1, 0], (ix, iy, partner)),
-            copy(chunk.at[spot_near], land_far.at[0], chunk_sems.at[0, 1], chunk_sems.at[1, 1], (ix, iy, near)),
-            copy(chunk.at[spot_far], land_far.at[1], chunk_sems.at[0, 2], chunk_sems.at[1, 2], (ix, iy, far)),
-        )
-
-    def column_copies():
-        return (
-            copy(column.at[pl.ds(theirs2, 2)], column_pair, column_sems.at[0, 0], column_sems.at[1, 0], (ix, iy, partner)),
-            copy(column.at[spot_near], column_far.at[0], column_sems.at[0, 1], column_sems.at[1, 1], (ix, iy, near)),
-            copy(column.at[spot_far], column_far.at[1], column_sems.at[0, 2], column_sems.at[1, 2], (ix, iy, far)),
-        )
-
-    def edge_copies(source, side, sems, to_x):
+    def chunk_copy(i):
+        t = others[i]
+        return copy(chunk.at[t], land.at[i], chunk_sems.at[0, i], chunk_sems.at[1, i], (ix, iy, t))
+
+    def column_copy(i):
+        t = others[i]
+        return copy(column.at[t], column_in.at[i], column_sems.at[0, i], column_sems.at[1, i], (ix, iy, t))
+
+    def edge_copy(source, side, sems, to_x, i):
         at = pl.ds(128 * side, 128)
-        return (
-            copy(source.at[pl.ds(mine2, 2)], halo.at[pl.ds(0, 2), :, at], sems.at[0, 0], sems.at[1, 0], (to_x, iy, it)),
-            copy(source.at[pl.ds(theirs2, 2)], halo.at[pl.ds(2, 2), :, at], sems.at[0, 1], sems.at[1, 1], (to_x, iy, partner)),
-            copy(source.at[spot_near], halo.at[4, :, at], sems.at[0, 2], sems.at[1, 2], (to_x, iy, near)),
-            copy(source.at[spot_far], halo.at[5, :, at], sems.at[0, 3], sems.at[1, 3], (to_x, iy, far)),
-        )
+        if i < 3:
+            t = others[i]
+            src, dst = source.at[t], halo.at[i, :, at]
+        else:
+            t, src, dst = it, source, halo_own.at[:, :, at]
+        return copy(src, dst, sems.at[0, i], sems.at[1, i], (to_x, iy, t))
 
     def rim_copies():
         return (
@@ -288,36 +279,37 @@
             (left_ok, copy(rim_out.at[1], rims.at[1], rim_sems.at[0, 1], rim_sems.at[1, 1], (ix, jnp.maximum(iy - 1, 0), it))),
         )
 
-    highs = edge_copies(edge_high, 0, high_sems, jnp.minimum(ix + 1, nx - 1))
-    lows = edge_copies(edge_low, 1, low_sems, jnp.maximum(ix - 1, 0))
-
-    def edges(index, act):
-        pl.when(can_up)(functools.partial(act, highs[index]))
-        pl.when(can_down)(functools.partial(act, lows[index]))
+    def high(i):
+        return edge_copy(edge_high, 0, high_sems, jnp.minimum(ix + 1, nx - 1), i)
+
+    def low(i):
+        return edge_copy(edge_low, 1, low_sems, jnp.maximum(ix - 1, 0), i)
+
+    def edges(i, act):
+        pl.when(can_up)(lambda: act(high(i)))
+        pl.when(can_down)(lambda: act(low(i)))
 
     def start(c):
         c.start()
 
     for ok, c in rim_copies():
         pl.when(ok)(functools.partial(start, c))
-    chunk_copies()[0].start()
-    edges(1, start)
-    edges(0, start)
-    chunk_copies()[1].start()
-    chunk_copies()[2].start()
-    edges(2, start)
     edges(3, start)
-
-    def halo_wait(index):
-        pl.when(can_down)(lambda: highs[index].wait_recv())
-        pl.when(can_up)(lambda: lows[index].wait_recv())
+    for i in (2, 1, 0):
+        chunk_copy(i).start()
+    for i in (2, 1, 0):
+        edges(i, start)
+
+    def halo_wait(i):
+        pl.when(can_down)(lambda: high(i).wait_recv())
+        pl.when(can_up)(lambda: low(i).wait_recv())
 
     pl.when(left_ok)(lambda: rim_copies()[0][1].wait_recv())
     pl.when(right_ok)(lambda: rim_copies()[1][1].wait_recv())
-    column[order[0]] = (rims[0].astype(f32) + left_of[1]).astype(b16)
-    column[order[nt - 1]] = (right_of[nt - 2] + rims[1].astype(f32)).astype(b16)
-    for c in column_copies():
-        c.start()
+    column[0] = (rims[0].astype(f32) + left_of[1]).astype(b16)
+    column[nt - 1] = (right_of[nt - 2] + rims[1].astype(f32)).astype(b16)
+    for i in (2, 1, 0):
+        column_copy(i).start()
 
     row, lane = iotas(lanes, lanes)
     gap = row - lane
@@ -358,104 +350,32 @@
         at = pl.ds(pl.multiple_of(block * snaps, snaps), snaps)
         coarse_ref[at], fine_ref[at] = values
 
-    def keep_side(block, values):
-        at = pl.ds(pl.multiple_of(block * snaps, snaps), snaps)
-        side_coarse[at], side_fine[at] = values
-
-    halo_wait(0)
-    keep(it, strain(chunk[mine2 + upper], halo[upper], column[mine2 + upper]))
-    keep_side(odd, strain(chunk[mine2 + 1 - upper], halo[1 - upper], column[mine2 + 1 - upper]))
-    chunk_copies()[0].wait_recv()
-    halo_wait(1)
-    column_copies()[0].wait_recv()
-    keep(partner, strain(land_pair[upper], halo[2 + upper], column_pair[upper]))
-    keep_side(1 - odd, strain(land_pair[1 - upper], halo[3 - upper], column_pair[1 - upper]))
-
-    pair = 2 * snaps
-    at = pl.ds(pl.multiple_of(upper * pair, pair), pair)
-    coarse, fine = coarse_ref[at], fine_ref[at]
-    gram = dot16(coarse, jnp.concatenate([coarse, fine], axis=0), (1, 1))
-    coarse, fine = side_coarse[...], side_fine[...]
-    gram = gram + dot16(coarse, jnp.concatenate([coarse, fine], axis=0), (1, 1))
-    skew = gram[:, pair:]
-    parts_pair[...] = (gram[:, :pair] + (skew + skew.T)).reshape(OWNERS, 8, pair)
-
-    near_rank = odd * plane + place
-    wide_rank = lax.rem(it + 3, 4) * plane + place
-
-    def pair_owner(k):
-        return (lax.div(lax.rem(k, plane), ny), lax.rem(lax.rem(k, plane), ny), 2 * upper + lax.div(k, plane))
-
-    def cross_owner(k):
-        return (lax.div(lax.rem(k, plane), ny), lax.rem(lax.rem(k, plane), ny), lax.rem(lax.div(k, plane) + 1, 4))
-
-    def scatter(level, act):
-        rank, owner, parts, landed = (
-            (near_rank, pair_owner, parts_pair, landed_pair),
-            (wide_rank, cross_owner, parts_cross, landed_cross),
-        )[level]
-        for j in range(OWNERS):
-            k = lax.rem(rank + j, OWNERS)
-            c = copy(parts.at[k], landed.at[rank], scatter_sems.at[level, j], scatter_in.at[level], owner(k))
-            if j:
-                act(c)
-            else:
-                pl.when(rank >= OWNERS)(functools.partial(act, c))
-
-    def spread(level, act):
-        rank, whole = ((near_rank, whole_pair), (wide_rank, whole_cross))[level]
-        slot = jnp.minimum(rank, OWNERS - 1) + (0 if level else OWNERS * upper)
-
+    halo_wait(3)
+    own = jnp.zeros((snaps, 2 * snaps), f32)
+    for q in range(nt):
+        coarse, fine = strain(chunk[q], halo_own[q], column[q])
+        own_coarse[q], own_fine[q] = coarse, fine
+        own = own + dot16(coarse, jnp.concatenate([coarse, fine], axis=0), (1, 1))
+    skew = own[:, snaps:]
+    own = own[:, :snaps] + (skew + skew.T)
+    half = snaps // 2
+    own_landed[place] = jnp.concatenate([own[:half], own[half:]], axis=1)
+
+    def own_copies(act):
         def body(j, carry):
+            t = lax.rem(place + j, plane)
             act(
                 copy(
-                    whole.at[slot], whole.at[slot], spread_sems.at[level, j], spread_in.at[level],
-                    device(lax.rem(me + j, devices)),
+                    own_landed.at[place], own_landed.at[place], own_sems.at[j], own_in.at[0],
+                    (lax.div(t, ny), lax.rem(t, ny), it),
                 )
             )
             return carry
 
-        @pl.when(rank < OWNERS)
-        def _():
-            lax.fori_loop(1, devices, body, 0)
-
-    def reduce(level):
-        rank, parts, landed = (
-            (near_rank, parts_pair, landed_pair),
-            (wide_rank, parts_cross, landed_cross),
-        )[level]
-        members = landed.shape[0]
-        slot = jnp.minimum(rank, OWNERS - 1)
-
-        @pl.when(rank < OWNERS)
-        def _():
-            landed[rank] = parts[slot]
-            some = landed.at[pl.ds(0, members - 1)]
-            copy(some, some, scatter_sems.at[level, 0], scatter_in.at[level], (ix, iy, partner)).wait_recv()
-            summed = jnp.sum(landed[...], axis=0)
-            if level:
-                whole_cross[slot] = summed
-            else:
-                whole_pair[OWNERS * upper + slot] = summed
-
-        spread(level, start)
-
-    scatter(0, start)
-
-    for i, t in enumerate((near, far)):
-        chunk_copies()[1 + i].wait_recv()
-        halo_wait(2 + i)
-        column_copies()[1 + i].wait_recv()
-        keep(t, strain(land_far[i], halo[4 + i], column_far[i]))
-    coarse, fine = coarse_ref[:pair], fine_ref[:pair]
-    coarse_high, fine_high = coarse_ref[pair:], fine_ref[pair:]
-    gram = dot16(coarse_high, jnp.concatenate([coarse, fine], axis=0), (1, 1))
-    crossed = gram[:, :pair] + (gram[:, pair:] + dot16(fine_high, coarse, (1, 1)))
-    parts_cross[...] = crossed.reshape(OWNERS, 8, pair)
-    scatter(1, start)
-    reduce(0)
-    reduce(1)
-
+        lax.fori_loop(1, plane, body, 0)
+
+    own_copies(start)
+    keep(it, (own_coarse[it], own_fine[it]))
     for c in loads[1:]:
         c.wait()
     first = eye(snaps, snaps) + seeds_first[...].astype(f32) * (0.5 / 512.0)
@@ -463,46 +383,123 @@
     turns = [
         stacked + seeds_merge[level].astype(f32) * (0.5 / (64.0 * 128.0**0.5)) for level in range(2)
     ]
-
-    @pl.when(near_rank < OWNERS)
-    def _():
-        some = whole_pair.at[pl.ds(0, 2 * OWNERS - 1)]
-        copy(some, some, spread_sems.at[0, 0], spread_in.at[0], (ix, iy, partner)).wait_recv()
-
-    @pl.when(near_rank >= OWNERS)
-    def _():
-        copy(whole_pair, whole_pair, spread_sems.at[0, 0], spread_in.at[0], (ix, iy, partner)).wait_recv()
-
-    pairs = [whole_pair[u * OWNERS : (u + 1) * OWNERS].reshape(pair, pair) for u in (0, 1)]
-    blocks = [
-        g[i * snaps : (i + 1) * snaps, i * snaps : (i + 1) * snaps] for g in pairs for i in (0, 1)
-    ]
-    coefs = first_level(blocks, first)
+    some = own_landed.at[pl.ds(0, plane - 1)]
+    copy(some, some, own_sems.at[0], own_in.at[0], (ix, iy, partner)).wait_recv()
+    packed = jnp.sum(own_landed[...], axis=0)
+    own = jnp.concatenate([packed[:, :snaps], packed[:, snaps:]], axis=0)
+    shared[it] = jnp.concatenate([first_level([own], first)[0], own], axis=1)
+
+    def share_copy(i):
+        return copy(shared.at[it], shared.at[it], share_sems.at[i], share_in.at[0], (ix, iy, others[i]))
+
+    for i in range(3):
+        share_copy(i).start()
+
+    for i in range(3):
+        chunk_copy(i).wait_recv()
+        halo_wait(i)
+        column_copy(i).wait_recv()
+        keep(others[i], strain(land[i], halo[i], column_in[i]))
+    pair = 2 * snaps
+    coarse, fine = coarse_ref[...], fine_ref[...]
+    rhs = jnp.concatenate([coarse[:pair], fine[:pair]], axis=0)
+    lower = dot16(coarse[snaps:], rhs, (1, 1))
+    lower = lower[:, :pair] + (lower[:, pair:] + dot16(fine[snaps:], coarse[:pair], (1, 1)))
+    rhs = jnp.concatenate([coarse[pair : pair + snaps], fine[pair : pair + snaps]], axis=0)
+    last = dot16(coarse[pair + snaps :], rhs, (1, 1))
+    last = last[:, :snaps] + (
+        last[:, snaps:] + dot16(fine[pair + snaps :], coarse[pair : pair + snaps], (1, 1))
+    )
+    rows = jnp.concatenate([lower[snaps:], jnp.concatenate([lower[:snaps, :snaps], last], axis=1)], axis=0)
+    parts[...] = rows.reshape(OWNERS, 8, pair)
+
+    rank = jnp.where(it == 0, 2, jnp.where(it == 3, 3, it - 1)) * plane + place
+    owner = rank < OWNERS
+    slot = jnp.minimum(rank, OWNERS - 1)
+
+    def scatter(act):
+        for j in range(OWNERS):
+            k = lax.rem(rank + j, OWNERS)
+            group, where = lax.div(k, plane), lax.rem(k, plane)
+            level = jnp.where(group == 2, 0, jnp.where(group == 3, 3, group + 1))
+            c = copy(
+                parts.at[k], landed.at[rank], scatter_sems.at[j], scatter_in.at[0],
+                (lax.div(where, ny), lax.rem(where, ny), level),
+            )
+            if j:
+                act(c)
+            else:
+                pl.when(jnp.logical_not(owner))(functools.partial(act, c))
+
+    def spread(act):
+        def body(j, carry):
+            act(
+                copy(
+                    whole.at[slot], whole.at[slot], spread_sems.at[j], spread_in.at[0],
+                    device(lax.rem(me + j, devices)),
+                )
+            )
+            return carry
+
+        @pl.when(owner)
+        def _():
+            lax.fori_loop(1, devices, body, 0)
+
+    scatter(start)
+
+    @pl.when(owner)
+    def _():
+        landed[rank] = parts[slot]
+        some = landed.at[pl.ds(0, devices - 1)]
+        copy(some, some, scatter_sems.at[0], scatter_in.at[0], (ix, iy, partner)).wait_recv()
+        whole[slot] = jnp.sum(landed[...], axis=0)
+
+    spread(start)
+    some = shared.at[pl.ds(0, nt - 1)]
+    copy(some, some, share_sems.at[0], share_in.at[0], (ix, iy, partner)).wait_recv()
+    coefs = [shared[b][:, :snaps] for b in range(nt)]
+    grams = [shared[b][:, snaps:] for b in range(nt)]
+
+    @pl.when(owner)
+    def _():
+        some = whole.at[pl.ds(0, OWNERS - 1)]
+        copy(some, some, spread_sems.at[0], spread_in.at[0], (ix, iy, partner)).wait_recv()
+
+    @pl.when(jnp.logical_not(owner))
+    def _():
+        copy(whole, whole, spread_sems.at[0], spread_in.at[0], (ix, iy, partner)).wait_recv()
+
+    rows = whole[...].reshape(OWNERS * 8, pair)
+    cross = rows[:pair]
+    pairs = []
+    for u in range(2):
+        mixed = rows[pair:, u * snaps : (u + 1) * snaps]
+        pairs.append(
+            jnp.concatenate(
+                [
+                    jnp.concatenate([grams[2 * u], mixed.T], axis=1),
+                    jnp.concatenate([mixed, grams[2 * u + 1]], axis=1),
+                ],
+                axis=0,
+            )
+        )
     weights = middle_level(pairs, (coefs[:2], coefs[2:]), turns[0])
-
-    @pl.when(wide_rank < OWNERS)
-    def _():
-        some = whole_cross.at[pl.ds(0, OWNERS - 1)]
-        copy(some, some, spread_sems.at[1, 0], spread_in.at[1], (ix, iy, partner)).wait_recv()
-
-    @pl.when(wide_rank >= OWNERS)
-    def _():
-        copy(whole_cross, whole_cross, spread_sems.at[1, 0], spread_in.at[1], (ix, iy, partner)).wait_recv()
-
-    weight_ref[...] = last_level(pairs, whole_cross[...].reshape(pair, pair), weights, turns[1])
+    weight_ref[...] = last_level(pairs, cross, weights, turns[1])
 
     def finish(c):
         c.wait_send()
 
     for ok, c in rim_copies():
         pl.when(ok)(functools.partial(finish, c))
-    for c in chunk_copies() + column_copies():
-        finish(c)
-    for index in range(4):
-        edges(index, finish)
-    for level in range(2):
-        scatter(level, finish)
-        spread(level, finish)
+    for i in range(3):
+        finish(chunk_copy(i))
+        finish(column_copy(i))
+        finish(share_copy(i))
+    for i in range(4):
+        edges(i, finish)
+    own_copies(finish)
+    scatter(finish)
+    spread(finish)
 
 
 def tail_kernel(weight_ref, coarse_ref, fine_ref, out_hbm, out, sem):
@@ -552,18 +549,16 @@
             pltpu.VMEM((nt, 16, rows3), b16),
             pltpu.VMEM((2, 16, rows3), b16),
             pltpu.VMEM((2, 16, rows3), b16),
-            pltpu.VMEM((2, rows3, lanes), b16),
-            pltpu.VMEM((2, rows3, lanes), b16),
-            pltpu.VMEM((2, 16, rows3), b16),
-            pltpu.VMEM((2, 16, rows3), b16),
-            pltpu.VMEM((6, rows3 // 2, 256), b16),
-            pltpu.VMEM((pair, 5 * lanes), b16),
-            pltpu.VMEM((pair, 5 * lanes), b16),
+            pltpu.VMEM((3, rows3, lanes), b16),
+            pltpu.VMEM((3, 16, rows3), b16),
+            pltpu.VMEM((nt, rows3 // 2, 256), b16),
+            pltpu.VMEM((3, rows3 // 2, 256), b16),
+            pltpu.VMEM((nt, width, 5 * lanes), b16),
+            pltpu.VMEM((nt, width, 5 * lanes), b16),
+            pltpu.VMEM((plane, width // 2, pair), f32),
+            pltpu.VMEM((nt, width, pair), f32),
             pltpu.VMEM((OWNERS, 8, pair), f32),
-            pltpu.VMEM((OWNERS, 8, pair), f32),
-            pltpu.VMEM((2 * plane, 8, pair), f32),
             pltpu.VMEM((nt * plane, 8, pair), f32),
-            pltpu.VMEM((2 * OWNERS, 8, pair), f32),
             pltpu.VMEM((OWNERS, 8, pair), f32),
             dma((3,)),
             dma((2, 3)),
@@ -571,10 +566,14 @@
             dma((2, 2)),
             dma((2, 4)),
             dma((2, 4)),
-            dma((2, OWNERS)),
-            dma((2,)),
-            dma((2, nt * plane)),
-            dma((2,)),
+            dma((plane,)),
+            dma((1,)),
+            dma((3,)),
+            dma((1,)),
+            dma((OWNERS,)),
+            dma((1,)),
+            dma((nt * plane,)),
+            dma((1,)),
         ],
         compiler_params=pltpu.CompilerParams(
             collective_id=0, has_side_effects=True, vmem_limit_bytes=40 * 2**20

time: 40.9 us -> 37.9 us (0.927)
  Pallas kernels: 40.8 us -> 37.7 us
    pallas_call x1, Pallas kernels: 39.5 us -> 36.5 us  [local(): pl.pallas_call(functools.partial(gather_kernel, quarter, nx, ny, nt), out...]
where the time goes in v2:
time: 37.9 us; the launch traced here: 37.8 us
  Pallas kernels  37.7 us (99%)
    pallas_call x1, Pallas kernels, local(): pl.pallas_call(functools.partial(gather_kernel, quarter, nx, ny, nt), out...  36.5 us
    pallas_call x1, Pallas kernels, local(): pl.pallas_call(tail_kernel, out_shape=jax.ShapeDtypeStruct((width * strip...  1.26 us

profile of v2, /device:TPU:0, one launch (start us, length us, event | category | flops | bytes accessed | tf_op | source)
XLA Modules:
  0.0 37.8 jit_solution(12919234644517338605)
XLA Ops:
  0.0 36.5 %gather.1 = (bf16[256,1280]{1,0:T(8,128)(2,1)S(1)}, bf16[256,1280]{1,0:T(8,128)(2,1)S(1)}, f32[64,256]{1,0:T(8,128)S(1)}) custom-call(bf16[3,64,4,256]{3,2,1,0:T(4,128)(2,1)} %velocity_hbm.1, s32[64,64]{1,0:T(8,128)} %first_hbm.1, s32[2,64,128]{2,1,0:T(8,128)} %bitcast.2), custom_call_target="tpu_custom_call" | custom-call | tf_op jit(solution)/shard_map/gather/pallas_call | solution.py:533
  36.5 1.3 %tail.1 = f32[1280,64]{1,0:T(8,128)} custom-call(f32[64,256]{1,0:T(8,128)S(1)} %get-tuple-element.8.weight_ref, bf16[256,1280]{1,0:T(8,128)(2,1)S(1)} %get-tuple-element.9.coarse_ref, bf16[256,1280]{1,0:T(8,128)(2,1)S(1)} %get-tuple-element.10.fine_ref), custom_call_target="tpu_custom_call" | custom-call | tf_op jit(solution)/shard_map/tail/pallas_call | solution.py:584

commit v3 on v2

--- a/solution.py
+++ b/solution.py
@@ -10,6 +10,7 @@
 HI = lax.Precision.HIGHEST
 MESH = pl.DeviceIdType.MESH
 OWNERS = 24
+LEAD = 8
 
 
 def mm(left, right, contract=(1, 0)):
@@ -107,23 +108,24 @@
     return [c * lax.rsqrt(total(g * ident) / width) for c, g in zip(solved, grams)]
 
 
-def middle_level(pairs, coefs, turn):
+def prepare(coefs, turn):
     width = turn.shape[0]
-    ident = eye(width, width)
+    lean = [mm(c, turn[:, i * width : (i + 1) * width], (0, 1)) for i, c in enumerate(coefs)]
+    return jnp.concatenate(lean, axis=0), [mm(c, c, (0, 0)) for c in coefs]
+
+
+def middle_level(pairs, ready):
+    width = pairs[0].shape[0] // 2
     reduced, sides, scales = [], [], []
-    for gram, (low, high) in zip(pairs, coefs):
-        lean = jnp.concatenate(
-            [mm(low, turn[:, :width], (0, 1)), mm(high, turn[:, width:], (0, 1))], axis=0
-        )
+    for gram, (lean, norms) in zip(pairs, ready):
         image = mm(lean, gram, (0, 0))
         reduced.append(mm(image, lean))
-        norms = [mm(c, c, (0, 0)) for c in (low, high)]
         sides.append(
             jnp.concatenate([mm(image[:, :width], norms[0]), mm(image[:, width:], norms[1])], axis=1)
         )
         trace = total(norms[0] * gram[:width, :width]) + total(norms[1] * gram[width:, width:])
         scales.append(lax.rsqrt(trace / (2 * width)))
-    inverses = eliminate(reduced, [ident] * len(pairs))
+    inverses = eliminate(reduced, [eye(width, width)] * len(pairs))
     return [mm(inv, s) * k for inv, s, k in zip(inverses, sides, scales)]
 
 
@@ -410,7 +412,7 @@
     last = last[:, :snaps] + (
         last[:, snaps:] + dot16(fine[pair + snaps :], coarse[pair : pair + snaps], (1, 1))
     )
-    rows = jnp.concatenate([lower[snaps:], jnp.concatenate([lower[:snaps, :snaps], last], axis=1)], axis=0)
+    rows = jnp.concatenate([jnp.concatenate([lower[:snaps, :snaps], last], axis=1), lower[snaps:]], axis=0)
     parts[...] = rows.reshape(OWNERS, 8, pair)
 
     rank = jnp.where(it == 0, 2, jnp.where(it == 3, 3, it - 1)) * plane + place
@@ -419,31 +421,32 @@
 
     def scatter(act):
         for j in range(OWNERS):
-            k = lax.rem(rank + j, OWNERS)
+            if j < LEAD:
+                k = lax.rem(place + j, LEAD)
+            else:
+                k = LEAD + lax.rem(place + j, OWNERS - LEAD)
             group, where = lax.div(k, plane), lax.rem(k, plane)
             level = jnp.where(group == 2, 0, jnp.where(group == 3, 3, group + 1))
             c = copy(
                 parts.at[k], landed.at[rank], scatter_sems.at[j], scatter_in.at[0],
                 (lax.div(where, ny), lax.rem(where, ny), level),
             )
-            if j:
-                act(c)
-            else:
-                pl.when(jnp.logical_not(owner))(functools.partial(act, c))
+            pl.when(rank != k)(functools.partial(act, c))
+
+    lead = slot < LEAD
 
     def spread(act):
-        def body(j, carry):
-            act(
-                copy(
-                    whole.at[slot], whole.at[slot], spread_sems.at[j], spread_in.at[0],
-                    device(lax.rem(me + j, devices)),
-                )
+        def body(t, carry):
+            c = copy(
+                whole.at[slot], whole.at[slot], spread_sems.at[t], spread_in.at[jnp.where(lead, 0, 1)],
+                device(t),
             )
+            pl.when(t != me)(functools.partial(act, c))
             return carry
 
         @pl.when(owner)
         def _():
-            lax.fori_loop(1, devices, body, 0)
+            lax.fori_loop(0, devices, body, 0)
 
     scatter(start)
 
@@ -460,20 +463,21 @@
     coefs = [shared[b][:, :snaps] for b in range(nt)]
     grams = [shared[b][:, snaps:] for b in range(nt)]
 
-    @pl.when(owner)
-    def _():
-        some = whole.at[pl.ds(0, OWNERS - 1)]
-        copy(some, some, spread_sems.at[0], spread_in.at[0], (ix, iy, partner)).wait_recv()
-
-    @pl.when(jnp.logical_not(owner))
-    def _():
-        copy(whole, whole, spread_sems.at[0], spread_in.at[0], (ix, iy, partner)).wait_recv()
-
-    rows = whole[...].reshape(OWNERS * 8, pair)
-    cross = rows[:pair]
+    ready = [prepare(coefs[2 * u : 2 * u + 2], turns[0]) for u in range(2)]
+
+    def arrived(part, first_piece, count, own_piece):
+        def wait(pieces):
+            some = whole.at[pl.ds(first_piece, pieces)]
+            copy(some, some, spread_sems.at[0], spread_in.at[part], (ix, iy, partner)).wait_recv()
+
+        pl.when(own_piece)(lambda: wait(count - 1))
+        pl.when(jnp.logical_not(own_piece))(lambda: wait(count))
+        return whole[first_piece : first_piece + count].reshape(count * 8, pair)
+
+    rows = arrived(0, 0, LEAD, jnp.logical_and(owner, lead))
     pairs = []
     for u in range(2):
-        mixed = rows[pair:, u * snaps : (u + 1) * snaps]
+        mixed = rows[:, u * snaps : (u + 1) * snaps]
         pairs.append(
             jnp.concatenate(
                 [
@@ -483,7 +487,8 @@
                 axis=0,
             )
         )
-    weights = middle_level(pairs, (coefs[:2], coefs[2:]), turns[0])
+    weights = middle_level(pairs, ready)
+    cross = arrived(1, LEAD, OWNERS - LEAD, jnp.logical_and(owner, jnp.logical_not(lead)))
     weight_ref[...] = last_level(pairs, cross, weights, turns[1])
 
     def finish(c):
@@ -573,7 +578,7 @@
             dma((OWNERS,)),
             dma((1,)),
             dma((nt * plane,)),
-            dma((1,)),
+            dma((2,)),
         ],
         compiler_params=pltpu.CompilerParams(
             collective_id=0, has_side_effects=True, vmem_limit_bytes=40 * 2**20

time: 37.9 us -> 36.6 us (0.966)
  Pallas kernels: 37.7 us -> 36.4 us
    pallas_call x1, Pallas kernels: 36.5 us -> 35.2 us  [local(): pl.pallas_call(functools.partial(gather_kernel, quarter, nx, ny, nt), out...]
where the time goes in v3:
time: 36.6 us; the launch traced here: 36.4 us
  Pallas kernels  36.4 us (99%)
    pallas_call x1, Pallas kernels, local(): pl.pallas_call(functools.partial(gather_kernel, quarter, nx, ny, nt), out...  35.2 us
    pallas_call x1, Pallas kernels, local(): pl.pallas_call(tail_kernel, out_shape=jax.ShapeDtypeStruct((width * strip...  1.26 us

profile of v3, /device:TPU:0, one launch (start us, length us, event | category | flops | bytes accessed | tf_op | source)
XLA Modules:
  0.0 36.4 jit_solution(2611043896211579614)
XLA Ops:
  0.0 35.2 %gather.1 = (bf16[256,1280]{1,0:T(8,128)(2,1)S(1)}, bf16[256,1280]{1,0:T(8,128)(2,1)S(1)}, f32[64,256]{1,0:T(8,128)S(1)}) custom-call(bf16[3,64,4,256]{3,2,1,0:T(4,128)(2,1)} %velocity_hbm.1, s32[64,64]{1,0:T(8,128)} %first_hbm.1, s32[2,64,128]{2,1,0:T(8,128)} %bitcast.2), custom_call_target="tpu_custom_call" | custom-call | tf_op jit(solution)/shard_map/gather/pallas_call | solution.py:538
  35.2 1.3 %tail.1 = f32[1280,64]{1,0:T(8,128)} custom-call(f32[64,256]{1,0:T(8,128)S(1)} %get-tuple-element.8.weight_ref, bf16[256,1280]{1,0:T(8,128)(2,1)S(1)} %get-tuple-element.9.coarse_ref, bf16[256,1280]{1,0:T(8,128)(2,1)S(1)} %get-tuple-element.10.fine_ref), custom_call_target="tpu_custom_call" | custom-call | tf_op jit(solution)/shard_map/tail/pallas_call | solution.py:589

commit v4 on v3

--- a/solution.py
+++ b/solution.py
@@ -199,13 +199,8 @@
     for t in others:
         greet((ix, iy, t))
     can_up, can_down = ix < nx - 1, ix > 0
-    for ok, step in ((can_up, 1), (can_down, -1)):
-        @pl.when(ok)
-        def _():
-            for t in others:
-                greet((ix + step, iy, t))
     lax.fori_loop(1, plane, greet_plane, 0)
-    expected = plane - 1 + 3 + jnp.where(can_up, 3, 0) + jnp.where(can_down, 3, 0)
+    expected = plane - 1 + 3
 
     right_ok, left_ok = iy + 1 < ny, iy > 0
 
@@ -270,10 +265,8 @@
         at = pl.ds(128 * side, 128)
         if i < 3:
             t = others[i]
-            src, dst = source.at[t], halo.at[i, :, at]
-        else:
-            t, src, dst = it, source, halo_own.at[:, :, at]
-        return copy(src, dst, sems.at[0, i], sems.at[1, i], (to_x, iy, t))
+            return copy(halo_own.at[t, :, at], halo.at[i, :, at], sems.at[0, i], sems.at[1, i], (ix, iy, t))
+        return copy(source, halo_own.at[:, :, at], sems.at[0, i], sems.at[1, i], (to_x, iy, it))
 
     def rim_copies():
         return (
@@ -288,8 +281,12 @@
         return edge_copy(edge_low, 1, low_sems, jnp.maximum(ix - 1, 0), i)
 
     def edges(i, act):
-        pl.when(can_up)(lambda: act(high(i)))
-        pl.when(can_down)(lambda: act(low(i)))
+        if i == 3:
+            pl.when(can_up)(lambda: act(high(i)))
+            pl.when(can_down)(lambda: act(low(i)))
+        else:
+            pl.when(can_down)(lambda: act(high(i)))
+            pl.when(can_up)(lambda: act(low(i)))
 
     def start(c):
         c.start()
@@ -297,11 +294,8 @@
     for ok, c in rim_copies():
         pl.when(ok)(functools.partial(start, c))
     edges(3, start)
-    for i in (2, 1, 0):
+    for i in (1, 2, 0):
         chunk_copy(i).start()
-    for i in (2, 1, 0):
-        edges(i, start)
-
     def halo_wait(i):
         pl.when(can_down)(lambda: high(i).wait_recv())
         pl.when(can_up)(lambda: low(i).wait_recv())
@@ -312,6 +306,9 @@
     column[nt - 1] = (right_of[nt - 2] + rims[1].astype(f32)).astype(b16)
     for i in (2, 1, 0):
         column_copy(i).start()
+    halo_wait(3)
+    for i in (2, 1, 0):
+        edges(i, start)
 
     row, lane = iotas(lanes, lanes)
     gap = row - lane
@@ -352,7 +349,6 @@
         at = pl.ds(pl.multiple_of(block * snaps, snaps), snaps)
         coarse_ref[at], fine_ref[at] = values
 
-    halo_wait(3)
     own = jnp.zeros((snaps, 2 * snaps), f32)
     for q in range(nt):
         coarse, fine = strain(chunk[q], halo_own[q], column[q])
@@ -378,6 +374,59 @@
 
     own_copies(start)
     keep(it, (own_coarse[it], own_fine[it]))
+    for i in range(3):
+        chunk_copy(i).wait_recv()
+        halo_wait(i)
+        column_copy(i).wait_recv()
+        keep(others[i], strain(land[i], halo[i], column_in[i]))
+    pair = 2 * snaps
+
+    def gram(high, low):
+        coarse, fine = coarse_ref[low], fine_ref[low]
+        size = coarse.shape[0]
+        both_low = dot16(coarse_ref[high], jnp.concatenate([coarse, fine], axis=0), (1, 1))
+        return both_low[:, :size] + (both_low[:, size:] + dot16(fine_ref[high], coarse, (1, 1)))
+
+    rank = jnp.where(it == 0, 2, jnp.where(it == 3, 3, it - 1)) * plane + place
+    owner = rank < OWNERS
+    slot = jnp.minimum(rank, OWNERS - 1)
+
+    def scatter(first_piece, last_piece, act):
+        for j in range(first_piece, last_piece):
+            if j < LEAD:
+                k = lax.rem(place + j, LEAD)
+            else:
+                k = LEAD + lax.rem(place + j, OWNERS - LEAD)
+            group, where = lax.div(k, plane), lax.rem(k, plane)
+            level = jnp.where(group == 2, 0, jnp.where(group == 3, 3, group + 1))
+            c = copy(
+                parts.at[k], landed.at[rank], scatter_sems.at[j], scatter_in.at[0],
+                (lax.div(where, ny), lax.rem(where, ny), level),
+            )
+            pl.when(rank != k)(functools.partial(act, c))
+
+    lead = slot < LEAD
+
+    def spread(act):
+        def body(t, carry):
+            c = copy(
+                whole.at[slot], whole.at[slot], spread_sems.at[t], spread_in.at[jnp.where(lead, 0, 1)],
+                device(t),
+            )
+            pl.when(t != me)(functools.partial(act, c))
+            return carry
+
+        @pl.when(owner)
+        def _():
+            lax.fori_loop(0, devices, body, 0)
+
+    blocks = [slice(b * snaps, (b + 1) * snaps) for b in range(nt)]
+    mixed = jnp.concatenate([gram(blocks[1], blocks[0]), gram(blocks[3], blocks[2])], axis=1)
+    parts[:LEAD] = mixed.reshape(LEAD, 8, pair)
+    scatter(0, LEAD, start)
+    parts[LEAD:] = gram(slice(pair, 2 * pair), slice(0, pair)).reshape(OWNERS - LEAD, 8, pair)
+    scatter(LEAD, OWNERS, start)
+
     for c in loads[1:]:
         c.wait()
     first = eye(snaps, snaps) + seeds_first[...].astype(f32) * (0.5 / 512.0)
@@ -396,59 +445,6 @@
 
     for i in range(3):
         share_copy(i).start()
-
-    for i in range(3):
-        chunk_copy(i).wait_recv()
-        halo_wait(i)
-        column_copy(i).wait_recv()
-        keep(others[i], strain(land[i], halo[i], column_in[i]))
-    pair = 2 * snaps
-    coarse, fine = coarse_ref[...], fine_ref[...]
-    rhs = jnp.concatenate([coarse[:pair], fine[:pair]], axis=0)
-    lower = dot16(coarse[snaps:], rhs, (1, 1))
-    lower = lower[:, :pair] + (lower[:, pair:] + dot16(fine[snaps:], coarse[:pair], (1, 1)))
-    rhs = jnp.concatenate([coarse[pair : pair + snaps], fine[pair : pair + snaps]], axis=0)
-    last = dot16(coarse[pair + snaps :], rhs, (1, 1))
-    last = last[:, :snaps] + (
-        last[:, snaps:] + dot16(fine[pair + snaps :], coarse[pair : pair + snaps], (1, 1))
-    )
-    rows = jnp.concatenate([jnp.concatenate([lower[:snaps, :snaps], last], axis=1), lower[snaps:]], axis=0)
-    parts[...] = rows.reshape(OWNERS, 8, pair)
-
-    rank = jnp.where(it == 0, 2, jnp.where(it == 3, 3, it - 1)) * plane + place
-    owner = rank < OWNERS
-    slot = jnp.minimum(rank, OWNERS - 1)
-
-    def scatter(act):
-        for j in range(OWNERS):
-            if j < LEAD:
-                k = lax.rem(place + j, LEAD)
-            else:
-                k = LEAD + lax.rem(place + j, OWNERS - LEAD)
-            group, where = lax.div(k, plane), lax.rem(k, plane)
-            level = jnp.where(group == 2, 0, jnp.where(group == 3, 3, group + 1))
-            c = copy(
-                parts.at[k], landed.at[rank], scatter_sems.at[j], scatter_in.at[0],
-                (lax.div(where, ny), lax.rem(where, ny), level),
-            )
-            pl.when(rank != k)(functools.partial(act, c))
-
-    lead = slot < LEAD
-
-    def spread(act):
-        def body(t, carry):
-            c = copy(
-                whole.at[slot], whole.at[slot], spread_sems.at[t], spread_in.at[jnp.where(lead, 0, 1)],
-                device(t),
-            )
-            pl.when(t != me)(functools.partial(act, c))
-            return carry
-
-        @pl.when(owner)
-        def _():
-            lax.fori_loop(0, devices, body, 0)
-
-    scatter(start)
 
     @pl.when(owner)
     def _():
@@ -503,7 +499,7 @@
     for i in range(4):
         edges(i, finish)
     own_copies(finish)
-    scatter(finish)
+    scatter(0, OWNERS, finish)
     spread(finish)
 
 

time: 36.6 us -> 36.2 us (0.989)
  Pallas kernels: 36.4 us -> 36 us
    pallas_call x1, Pallas kernels: 35.2 us -> 34.8 us  [local(): pl.pallas_call(functools.partial(gather_kernel, quarter, nx, ny, nt), out...]
where the time goes in v4:
time: 36.2 us; the launch traced here: 36 us
  Pallas kernels  36 us (99%)
    pallas_call x1, Pallas kernels, local(): pl.pallas_call(functools.partial(gather_kernel, quarter, nx, ny, nt), out...  34.8 us
    pallas_call x1, Pallas kernels, local(): pl.pallas_call(tail_kernel, out_shape=jax.ShapeDtypeStruct((width * strip...  1.26 us

profile of v4, /device:TPU:0, one launch (start us, length us, event | category | flops | bytes accessed | tf_op | source)
XLA Modules:
  0.0 36.0 jit_solution(8529203441407976244)
XLA Ops:
  0.0 34.8 %gather.1 = (bf16[256,1280]{1,0:T(8,128)(2,1)S(1)}, bf16[256,1280]{1,0:T(8,128)(2,1)S(1)}, f32[64,256]{1,0:T(8,128)S(1)}) custom-call(bf16[3,64,4,256]{3,2,1,0:T(4,128)(2,1)} %velocity_hbm.1, s32[64,64]{1,0:T(8,128)} %first_hbm.1, s32[2,64,128]{2,1,0:T(8,128)} %bitcast.2), custom_call_target="tpu_custom_call" | custom-call | tf_op jit(solution)/shard_map/gather/pallas_call | solution.py:534
  34.8 1.3 %tail.1 = f32[1280,64]{1,0:T(8,128)} custom-call(f32[64,256]{1,0:T(8,128)S(1)} %get-tuple-element.8.weight_ref, bf16[256,1280]{1,0:T(8,128)(2,1)S(1)} %get-tuple-element.9.coarse_ref, bf16[256,1280]{1,0:T(8,128)(2,1)S(1)} %get-tuple-element.10.fine_ref), custom_call_target="tpu_custom_call" | custom-call | tf_op jit(solution)/shard_map/tail/pallas_call | solution.py:585

commit v5 on v4

--- a/solution.py
+++ b/solution.py
@@ -149,7 +149,7 @@
     velocity_hbm, first_hbm, merge_hbm,
     coarse_ref, fine_ref, weight_ref,
     velocity, seeds_first, seeds_merge, chunk, edge_low, edge_high, column, rim_out,
-    rims, land, column_in, halo_own, halo,
+    rims, land, column_in, halo_own, halo, passed,
     own_coarse, own_fine, own_landed, shared, parts, landed, whole,
     load_sems, chunk_sems, column_sems, rim_sems, low_sems, high_sems,
     own_sems, own_in, share_sems, share_in, scatter_sems, scatter_in, spread_sems, spread_in,
@@ -208,11 +208,13 @@
     def _():
         halo[:, :, :128] = jnp.zeros((3, half3, 128), b16)
         halo_own[:, :, :128] = jnp.zeros((nt, half3, 128), b16)
+        passed[0] = jnp.zeros((rows3, 128), b16)
 
     @pl.when(jnp.logical_not(can_up))
     def _():
         halo[:, :, 128:] = jnp.zeros((3, half3, 128), b16)
         halo_own[:, :, 128:] = jnp.zeros((nt, half3, 128), b16)
+        passed[1] = jnp.zeros((rows3, 128), b16)
 
     @pl.when(jnp.logical_not(left_ok))
     def _():
@@ -263,6 +265,9 @@
 
     def edge_copy(source, side, sems, to_x, i):
         at = pl.ds(128 * side, 128)
+        if i == 1:
+            src = land.at[1, :, pl.ds((1 - side) * (lanes - 128), 128)]
+            return copy(src, passed.at[side], sems.at[0, i], sems.at[1, i], (to_x, iy, it))
         if i < 3:
             t = others[i]
             return copy(halo_own.at[t, :, at], halo.at[i, :, at], sems.at[0, i], sems.at[1, i], (ix, iy, t))
@@ -281,7 +286,7 @@
         return edge_copy(edge_low, 1, low_sems, jnp.maximum(ix - 1, 0), i)
 
     def edges(i, act):
-        if i == 3:
+        if i in (1, 3):
             pl.when(can_up)(lambda: act(high(i)))
             pl.when(can_down)(lambda: act(low(i)))
         else:
@@ -294,7 +299,7 @@
     for ok, c in rim_copies():
         pl.when(ok)(functools.partial(start, c))
     edges(3, start)
-    for i in (1, 2, 0):
+    for i in (1, 0, 2):
         chunk_copy(i).start()
     def halo_wait(i):
         pl.when(can_down)(lambda: high(i).wait_recv())
@@ -307,7 +312,7 @@
     for i in (2, 1, 0):
         column_copy(i).start()
     halo_wait(3)
-    for i in (2, 1, 0):
+    for i in (2, 0):
         edges(i, start)
 
     row, lane = iotas(lanes, lanes)
@@ -334,10 +339,21 @@
         (row < cells_x) & (lane == row * quarter),
     )
 
+    row, lane = iotas(256, lanes)
+    k = lax.rem(row, 128)
+    beside = signed_half(
+        (row >= 128) & (k < quarter) & (lane == k + lanes - quarter),
+        (row < 128) & (lane == k - (128 - quarter)),
+    )
+
     def strain(block, border, sides):
         inner = dot16(block, both)
-        across = dot16(border, outer)
-        dx = inner[:, :lanes] + jnp.concatenate([across[:, :lanes], across[:, lanes:]], axis=0)
+        if border is None:
+            across = dot16(jnp.concatenate([passed[0], passed[1]], axis=1), beside)
+        else:
+            across = dot16(border, outer)
+            across = jnp.concatenate([across[:, :lanes], across[:, lanes:]], axis=0)
+        dx = inner[:, :lanes] + across
         dy = inner[:, lanes:] + dot16(sides, rim, (0, 0))
         ux, vx, wx = (dx[i * snaps : (i + 1) * snaps] for i in range(3))
         uy, vy, wy = (dy[i * snaps : (i + 1) * snaps] for i in range(3))
@@ -374,11 +390,14 @@
 
     own_copies(start)
     keep(it, (own_coarse[it], own_fine[it]))
-    for i in range(3):
-        chunk_copy(i).wait_recv()
+    chunk_copy(1).wait_recv()
+    edges(1, start)
+    for i in (0, 2, 1):
+        if i != 1:
+            chunk_copy(i).wait_recv()
         halo_wait(i)
         column_copy(i).wait_recv()
-        keep(others[i], strain(land[i], halo[i], column_in[i]))
+        keep(others[i], strain(land[i], None if i == 1 else halo[i], column_in[i]))
     pair = 2 * snaps
 
     def gram(high, low):
@@ -469,6 +488,21 @@
         pl.when(own_piece)(lambda: wait(count - 1))
         pl.when(jnp.logical_not(own_piece))(lambda: wait(count))
         return whole[first_piece : first_piece + count].reshape(count * 8, pair)
+
+    def finish(c):
+        c.wait_send()
+
+    for ok, c in rim_copies():
+        pl.when(ok)(functools.partial(finish, c))
+    for i in range(3):
+        finish(chunk_copy(i))
+        finish(column_copy(i))
+        finish(share_copy(i))
+    for i in range(4):
+        edges(i, finish)
+    own_copies(finish)
+    scatter(0, OWNERS, finish)
+    spread(finish)
 
     rows = arrived(0, 0, LEAD, jnp.logical_and(owner, lead))
     pairs = []
@@ -486,21 +520,6 @@
     weights = middle_level(pairs, ready)
     cross = arrived(1, LEAD, OWNERS - LEAD, jnp.logical_and(owner, jnp.logical_not(lead)))
     weight_ref[...] = last_level(pairs, cross, weights, turns[1])
-
-    def finish(c):
-        c.wait_send()
-
-    for ok, c in rim_copies():
-        pl.when(ok)(functools.partial(finish, c))
-    for i in range(3):
-        finish(chunk_copy(i))
-        finish(column_copy(i))
-        finish(share_copy(i))
-    for i in range(4):
-        edges(i, finish)
-    own_copies(finish)
-    scatter(0, OWNERS, finish)
-    spread(finish)
 
 
 def tail_kernel(weight_ref, coarse_ref, fine_ref, out_hbm, out, sem):
@@ -554,6 +573,7 @@
             pltpu.VMEM((3, 16, rows3), b16),
             pltpu.VMEM((nt, rows3 // 2, 256), b16),
             pltpu.VMEM((3, rows3 // 2, 256), b16),
+            pltpu.VMEM((2, rows3, 128), b16),
             pltpu.VMEM((nt, width, 5 * lanes), b16),
             pltpu.VMEM((nt, width, 5 * lanes), b16),
             pltpu.VMEM((plane, width // 2, pair), f32),

time: 36.2 us -> 34.9 us (0.964)
  Pallas kernels: 36 us -> 34.7 us
    pallas_call x1, Pallas kernels: 34.8 us -> 33.5 us  [local(): pl.pallas_call(functools.partial(gather_kernel, quarter, nx, ny, nt), out...]
where the time goes in v5:
time: 34.9 us; the launch traced here: 34.7 us
  Pallas kernels  34.7 us (99%)
    pallas_call x1, Pallas kernels, local(): pl.pallas_call(functools.partial(gather_kernel, quarter, nx, ny, nt), out...  33.5 us
    pallas_call x1, Pallas kernels, local(): pl.pallas_call(tail_kernel, out_shape=jax.ShapeDtypeStruct((width * strip...  1.26 us

profile of v5, /device:TPU:0, one launch (start us, length us, event | category | flops | bytes accessed | tf_op | source)
XLA Modules:
  0.0 34.7 jit_solution(12214232188221047692)
XLA Ops:
  0.0 33.5 %gather.1 = (bf16[256,1280]{1,0:T(8,128)(2,1)S(1)}, bf16[256,1280]{1,0:T(8,128)(2,1)S(1)}, f32[64,256]{1,0:T(8,128)S(1)}) custom-call(bf16[3,64,4,256]{3,2,1,0:T(4,128)(2,1)} %velocity_hbm.1, s32[64,64]{1,0:T(8,128)} %first_hbm.1, s32[2,64,128]{2,1,0:T(8,128)} %bitcast.2), custom_call_target="tpu_custom_call" | custom-call | tf_op jit(solution)/shard_map/gather/pallas_call | solution.py:553
  33.5 1.3 %tail.1 = f32[1280,64]{1,0:T(8,128)} custom-call(f32[64,256]{1,0:T(8,128)S(1)} %get-tuple-element.8.weight_ref, bf16[256,1280]{1,0:T(8,128)(2,1)S(1)} %get-tuple-element.9.coarse_ref, bf16[256,1280]{1,0:T(8,128)(2,1)S(1)} %get-tuple-element.10.fine_ref), custom_call_target="tpu_custom_call" | custom-call | tf_op jit(solution)/shard_map/tail/pallas_call | solution.py:605

commit v6 on v5

--- a/solution.py
+++ b/solution.py
@@ -48,51 +48,74 @@
     return (0.5 * plus.astype(jnp.float32) - 0.5 * minus.astype(jnp.float32)).astype(jnp.bfloat16)
 
 
+def tree(terms):
+    while len(terms) > 1:
+        terms = [a + b for a, b in zip(terms[::2], terms[1::2])]
+    return terms[0]
+
+
 def eliminate(mats, sides):
     n = mats[0].shape[0]
-    batch = len(mats)
-    tiles = n // 8
-    width = 2 * n
-    work = [
-        [jnp.concatenate([m, s], axis=1)[8 * i : 8 * i + 8] for i in range(tiles)]
-        for m, s in zip(mats, sides)
-    ]
+    tiles, width, single = n // 8, 2 * n, len(mats) == 1
+    halves = [mats + sides] if single else [mats, sides]
+    work = [[jnp.concatenate(h, axis=1)[8 * i : 8 * i + 8] for i in range(tiles)] for h in halves]
     sub = lax.broadcasted_iota(jnp.int32, (8, width), 0)
-    done = [[None] * tiles for _ in range(batch)]
+    left = lax.broadcasted_iota(jnp.int32, (8, width), 1) < n
+
+    def spread(tile, row):
+        return jnp.broadcast_to(tile[row : row + 1], (8, width))
+
+    def column(i, j):
+        tile = work[0][i]
+        value = jnp.broadcast_to(tile[:, j : j + 1], (8, width))
+        if single:
+            return value
+        return jnp.where(left, value, jnp.broadcast_to(tile[:, n + j : n + j + 1], (8, width)))
+
+    done = [[None] * tiles for _ in work]
+    now = [column(0, k) for k in range(8)]
     for p in range(tiles):
-        cols = [
-            [
-                [
-                    jnp.broadcast_to(work[b][i][:, 8 * p + k : 8 * p + k + 1], (8, width))
-                    for i in range(p, tiles)
-                ]
-                for k in range(8)
-            ]
-            for b in range(batch)
-        ]
-        for b in range(batch):
-            head = work[b][p]
-            rest = [work[b][i] for i in range(p + 1, tiles)]
-            scales = jnp.zeros((8, width), jnp.float32)
-            for k in range(8):
-                pivot = cols[b][k][0][k : k + 1]
-                inv = 1.0 / pivot
-                scales = jnp.where(sub == k, jnp.broadcast_to(inv, (8, width)), scales)
-                row = head[k : k + 1] * inv
-                across = [cols[b][j][0][k : k + 1] * inv for j in range(k + 1, 8)]
-                below = jnp.where(sub > k, cols[b][k][0], 0.0)
-                head = head - below * row
+        more = p + 1 < tiles
+        if more:
+            below = [column(p + 1, 8 * p + k) for k in range(8)]
+            head = [column(p, 8 * p + 8 + k) for k in range(8)]
+            foot = [column(p + 1, 8 * p + 8 + k) for k in range(8)]
+        raw = [[column(i, 8 * p + k) for k in range(8)] for i in range(p + 2, tiles)]
+        scales = None
+        for k in range(8):
+            pivot = spread(now[k], k)
+            inv = 1.0 / pivot
+            root = lax.rsqrt(pivot)
+            rows = [spread(w[p], k) for w in work]
+            for d, row in zip(done, rows):
+                d[p] = row * root if k == 0 else jnp.where(sub >= k, row * root, d[p])
+            scales = inv if k == 0 else jnp.where(sub >= k, inv, scales)
+            across = [spread(now[j], k) for j in range(k + 1, 8)]
+            f = jnp.where(sub == k, 0.0, now[k]) * inv
+            for w, row in zip(work, rows):
+                w[p] = w[p] - f * row
+            for j in range(k + 1, 8):
+                now[j] = now[j] - f * across[j - k - 1]
+            if more:
+                ahead = [spread(h, k) for h in head]
+                g = below[k] * inv
+                for w, row in zip(work, rows):
+                    w[p + 1] = w[p + 1] - g * row
                 for j in range(k + 1, 8):
-                    cols[b][j][0] = cols[b][j][0] - below * across[j - k - 1]
-                for i in range(1, tiles - p):
-                    factor = cols[b][k][i]
-                    rest[i - 1] = rest[i - 1] - factor * row
-                    for j in range(k + 1, 8):
-                        cols[b][j][i] = cols[b][j][i] - factor * across[j - k - 1]
-            done[b][p] = head * jnp.sqrt(scales)
-            for i in range(p + 1, tiles):
-                work[b][i] = rest[i - p - 1]
-    return [jnp.concatenate(done[b], axis=0)[:, n:] for b in range(batch)]
+                    below[j] = below[j] - g * across[j - k - 1]
+                for j in range(8):
+                    foot[j] = foot[j] - g * ahead[j]
+                    if k < 7:
+                        head[j] = head[j] - f * ahead[j]
+        for w in work:
+            full = w[p] * scales
+            spreads = [spread(full, k) for k in range(8)]
+            for i in range(p + 2, tiles):
+                w[i] = w[i] - tree([raw[i - p - 2][k] * spreads[k] for k in range(8)])
+        if more:
+            now = foot
+    out = [jnp.concatenate(d, axis=0) for d in done]
+    return [out[0][:, n:]] if single else [out[1][:, :n], out[1][:, n:]]
 
 
 def total(entries):
@@ -298,9 +321,10 @@
 
     for ok, c in rim_copies():
         pl.when(ok)(functools.partial(start, c))
+    chunk_copy(1).start()
     edges(3, start)
-    for i in (1, 0, 2):
-        chunk_copy(i).start()
+    chunk_copy(0).start()
+    chunk_copy(2).start()
     def halo_wait(i):
         pl.when(can_down)(lambda: high(i).wait_recv())
         pl.when(can_up)(lambda: low(i).wait_recv())

time: 34.9 us -> 34.5 us (0.989)
    pallas_call x1, Pallas kernels: 33.5 us -> 33.1 us  [local(): pl.pallas_call(functools.partial(gather_kernel, quarter, nx, ny, nt), out...]
where the time goes in v6:
time: 34.5 us; the launch traced here: 34.4 us
  Pallas kernels  34.4 us (100%)
    pallas_call x1, Pallas kernels, local(): pl.pallas_call(functools.partial(gather_kernel, quarter, nx, ny, nt), out...  33.1 us
    pallas_call x1, Pallas kernels, local(): pl.pallas_call(tail_kernel, out_shape=jax.ShapeDtypeStruct((width * strip...  1.27 us

profile of v6, /device:TPU:0, one launch (start us, length us, event | category | flops | bytes accessed | tf_op | source)
XLA Modules:
  0.0 34.4 jit_solution(9947118838672145884)
XLA Ops:
  0.0 33.1 %gather.1 = (bf16[256,1280]{1,0:T(8,128)(2,1)S(1)}, bf16[256,1280]{1,0:T(8,128)(2,1)S(1)}, f32[64,256]{1,0:T(8,128)S(1)}) custom-call(bf16[3,64,4,256]{3,2,1,0:T(4,128)(2,1)} %velocity_hbm.1, s32[64,64]{1,0:T(8,128)} %first_hbm.1, s32[2,64,128]{2,1,0:T(8,128)} %bitcast.2), custom_call_target="tpu_custom_call" | custom-call | tf_op jit(solution)/shard_map/gather/pallas_call | solution.py:577
  33.1 1.3 %tail.1 = f32[1280,64]{1,0:T(8,128)} custom-call(f32[64,256]{1,0:T(8,128)S(1)} %get-tuple-element.8.weight_ref, bf16[256,1280]{1,0:T(8,128)(2,1)S(1)} %get-tuple-element.9.coarse_ref, bf16[256,1280]{1,0:T(8,128)(2,1)S(1)} %get-tuple-element.10.fine_ref), custom_call_target="tpu_custom_call" | custom-call | tf_op jit(solution)/shard_map/tail/pallas_call | solution.py:629

commit v7 on v6

--- a/solution.py
+++ b/solution.py
@@ -205,9 +205,6 @@
             ((velocity_hbm, velocity), (first_hbm, seeds_first), (merge_hbm, seeds_merge))
         )
     ]
-    for c in loads:
-        c.start()
-
     barrier = pltpu.get_barrier_semaphore()
 
     def greet(target):
@@ -223,6 +220,8 @@
         greet((ix, iy, t))
     can_up, can_down = ix < nx - 1, ix > 0
     lax.fori_loop(1, plane, greet_plane, 0)
+    for c in loads:
+        c.start()
     expected = plane - 1 + 3
 
     right_ok, left_ok = iy + 1 < ny, iy > 0

time: 34.5 us -> 34.5 us (level)
  no operation moved by 1% of the time
where the time goes in v7:
time: 34.5 us; the launch traced here: 34.4 us
  Pallas kernels  34.4 us (100%)
    pallas_call x1, Pallas kernels, local(): pl.pallas_call(functools.partial(gather_kernel, quarter, nx, ny, nt), out...  33.1 us
    pallas_call x1, Pallas kernels, local(): pl.pallas_call(tail_kernel, out_shape=jax.ShapeDtypeStruct((width * strip...  1.26 us

profile of v7, /device:TPU:0, one launch (start us, length us, event | category | flops | bytes accessed | tf_op | source)
XLA Modules:
  0.0 34.4 jit_solution(9803128640908436096)
XLA Ops:
  0.0 33.1 %gather.1 = (bf16[256,1280]{1,0:T(8,128)(2,1)S(1)}, bf16[256,1280]{1,0:T(8,128)(2,1)S(1)}, f32[64,256]{1,0:T(8,128)S(1)}) custom-call(bf16[3,64,4,256]{3,2,1,0:T(4,128)(2,1)} %velocity_hbm.1, s32[64,64]{1,0:T(8,128)} %first_hbm.1, s32[2,64,128]{2,1,0:T(8,128)} %bitcast.2), custom_call_target="tpu_custom_call" | custom-call | tf_op jit(solution)/shard_map/gather/pallas_call | solution.py:576
  33.1 1.3 %tail.1 = f32[1280,64]{1,0:T(8,128)} custom-call(f32[64,256]{1,0:T(8,128)S(1)} %get-tuple-element.8.weight_ref, bf16[256,1280]{1,0:T(8,128)(2,1)S(1)} %get-tuple-element.9.coarse_ref, bf16[256,1280]{1,0:T(8,128)(2,1)S(1)} %get-tuple-element.10.fine_ref), custom_call_target="tpu_custom_call" | custom-call | tf_op jit(solution)/shard_map/tail/pallas_call | solution.py:628
